TPU v7x, 256 devices: a whole 4x4x8 slice. The times are simulated.
256 devices in a mesh: gx: 32 (over z_hi, x, y), gy: 8 (over z_lo, core).
Axes of the slice: x: 4, y: 4, z: 8 (z_hi: 2, z_lo: 4; z = z_hi * 4 + z_lo), core: 2. Of those that a mesh axis runs over, the one named last changes fastest.
Arguments:
- offsets: float32 [32, 8, 3, 8192], P('gx', 'gy'), may hold values from -0.5 to 0.5
- line: float32 [32, 8, 3, 8192], P('gx', 'gy'), may hold values from -6 to 6
- burgers_kind: int32 [32, 8, 8192], P('gx', 'gy'), may hold values from 0 to 7
- seg_cell: int32 [32, 8, 8192], P('gx', 'gy'), may hold values from 0 to 63
- end_node: int32 [32, 8, 2, 8192], P('gx', 'gy'), may hold values from 0 to 8191
- end_owner: int32 [32, 8, 2, 8192], P('gx', 'gy'), may hold values from 0 to 4
- drag: float32 [32, 8, 8192], P('gx', 'gy'), may hold values from 0.5 to 4
- applied: float32 [6], replicated, may hold values from -4 to 4
- pair_list: int32 [32, 8, 2, 1024], P('gx', 'gy'), may hold values from 0 to 191, as said below
- ghost_x_list: int32 [32, 8, 2, 32], P('gx', 'gy'), may hold values from 0 to 63
- ghost_y_list: int32 [32, 8, 2, 32], P('gx', 'gy'), may hold values from 0 to 127
Outputs:
- velocity: float32 [32, 8, 3, 8192], P('gx', 'gy')
Inputs may be any that keep to these rules, and one draw needn't show every extreme that they name: `pair_list`: per domain the real pairs (target below 64) come first and the remaining slots are padding with target 64 and source 0; the number of real pairs is a multiple of 256, at least 512, and at least one domain has 1024.
All inputs are finite; a program needn't handle non-finite values.
Results may differ from a plain program's by a relative error of at most 0.0003.
Values sent between devices are 32-bit elements; how exact they have to be, the bound alone decides.
A program may use at most 128 MiB of HBM per device.

v0:
```python
import math

import jax
import jax.numpy as jnp
from jax import lax
from jax.sharding import PartitionSpec as P

SEG = 128
CCX = 1
CCY = 4
NCZ = 16


CORE_SQUARE = 0.25
SHEAR_TERM = 1.0 / (8.0 * math.pi)
BULK_TERM = 1.0 / (4.0 * math.pi * 0.7)
CORE_LENGTH = 1.0
COMPONENTS = ((0, 0), (1, 1), (2, 2), (0, 1), (0, 2), (1, 2))
pair_group = 8
far_group = 16


def with_halo(cells, sides, width):
    for axis, dim in sides:
        count = lax.axis_size(axis)
        head = lax.slice_in_dim(cells, 0, width, axis=dim)
        tail = lax.slice_in_dim(cells, cells.shape[dim] - width, cells.shape[dim], axis=dim)
        cells = jnp.concatenate(
            [
                lax.ppermute(tail, axis, [(i, (i + 1) % count) for i in range(count)]),
                cells,
                lax.ppermute(head, axis, [((i + 1) % count, i) for i in range(count)]),
            ],
            axis=dim,
        )
    return cells


def point_stress(rx, ry, rz, moment):
    ra_square = rx * rx + ry * ry + rz * rz + CORE_SQUARE
    inv_one = 1.0 / jnp.sqrt(ra_square)
    inv_three = inv_one * inv_one * inv_one
    inv_five = inv_three * inv_one * inv_one
    slope = -(2.0 * inv_three + 3.0 * CORE_SQUARE * inv_five)
    dist = (rx, ry, rz)
    grad = (slope * rx, slope * ry, slope * rz)
    amat = [[moment[3 * first + second] for second in range(3)] for first in range(3)]
    curl = (amat[1][2] - amat[2][1], amat[2][0] - amat[0][2], amat[0][1] - amat[1][0])
    crossed = [
        [
            grad[(row + 1) % 3] * amat[(row + 2) % 3][col]
            - grad[(row + 2) % 3] * amat[(row + 1) % 3][col]
            for col in range(3)
        ]
        for row in range(3)
    ]
    curl_dist = curl[0] * rx + curl[1] * ry + curl[2] * rz
    curl_grad = curl[0] * grad[0] + curl[1] * grad[1] + curl[2] * grad[2]
    result = []
    for row, col in COMPONENTS:
        first_term = crossed[row][col] + crossed[col][row]
        second_term = (
            -(curl[row] * dist[col] + curl[col] * dist[row]) * inv_three
            + 3.0 * curl_dist * dist[row] * dist[col] * inv_five
        )
        if row == col:
            second_term = second_term - curl_dist * inv_three - curl_grad
        result.append(-SHEAR_TERM * first_term - BULK_TERM * second_term)
    return result


def local_rows(cell):
    return (cell // (CCY * NCZ), cell // NCZ % CCY, cell % NCZ)


def segment_data(offsets, line, kind, cell):
    position = jnp.stack(local_rows(cell), 0).astype(jnp.float32) + 0.5 + offsets
    burgers = jnp.stack(
        [1.0 - 2.0 * (kind // 2**bit % 2).astype(jnp.float32) for bit in range(3)], 0
    )
    data = jnp.concatenate([position, line, burgers], 0)
    return data.reshape(9, -1, SEG)


def pick_blocks(buffer, lists):
    return jnp.moveaxis(buffer[:, lists], 1, 0)


def group_stress(owned, ghosts, targets, sources):
    blocks = owned.shape[1]
    target_data = owned[:, jnp.clip(targets, 0, blocks - 1)]
    source_data = ghosts[:, sources]
    rx = target_data[0][:, :, None] - source_data[0][:, None, :]
    ry = target_data[1][:, :, None] - source_data[1][:, None, :]
    rz = target_data[2][:, :, None] - source_data[2][:, None, :]
    moment = [
        source_data[6 + first][:, None, :] * source_data[3 + second][:, None, :]
        for first in range(3)
        for second in range(3)
    ]
    parts = point_stress(rx, ry, rz, moment)
    return jnp.stack([jnp.sum(piece, axis=-1) for piece in parts], 0)


def cell_coords(device_x, device_y, cell):
    lower_x, lower_y, lower_z = local_rows(cell)
    coord_x = (device_x * CCX + lower_x).astype(jnp.float32)
    coord_y = (device_y * CCY + lower_y).astype(jnp.float32)
    coord_z = lower_z.astype(jnp.float32)
    return tuple(jnp.broadcast_arrays(coord_x, coord_y, coord_z))


def wrapped(diff, extent):
    half = extent / 2.0
    return jnp.where(diff > half, diff - extent, jnp.where(diff < -half, diff + extent, diff))


def pair_far(target_x, target_y, target_z, source_x, source_y, source_z, moment, extents):
    delta_x = wrapped(target_x[:, None] - source_x.reshape(1, -1), extents[0])
    delta_y = wrapped(target_y[:, None] - source_y.reshape(1, -1), extents[1])
    delta_z = wrapped(target_z[:, None] - source_z.reshape(1, -1), extents[2])
    nearby = (jnp.abs(delta_x) <= 1.0) & (jnp.abs(delta_y) <= 1.0) & (jnp.abs(delta_z) <= 1.0)
    weight = 1.0 - nearby.astype(jnp.float32)
    parts = point_stress(delta_x, delta_y, delta_z, moment)
    return jnp.stack([jnp.sum(piece * weight, axis=-1) for piece in parts], 0)


def far_stress(moments, device_x, device_y, grid_x, grid_y):
    count = moments.shape[2]
    cells = jnp.arange(count, dtype=jnp.int32)
    target_x, target_y, target_z = cell_coords(device_x, device_y, cells)
    extents = (float(CCX * grid_x), float(CCY * grid_y), float(NCZ))

    def far_step(total, index):
        first = index * far_group
        block = lax.dynamic_slice_in_dim(moments, first, far_group, 0)
        devices = first + jnp.arange(far_group, dtype=jnp.int32)
        source_x, source_y, source_z = cell_coords(
            devices[:, None] // grid_y, devices[:, None] % grid_y, cells[None, :]
        )
        moment = [block[:, entry, :].reshape(1, -1) for entry in range(9)]
        return (
            total
            + pair_far(target_x, target_y, target_z, source_x, source_y, source_z, moment, extents),
            None,
        )

    start = jnp.zeros((6, count), jnp.float32)
    turns = grid_x * grid_y // far_group
    return lax.scan(far_step, start, jnp.arange(turns, dtype=jnp.int32))[0]


def cell_moments(data, cell, count):
    flat = data.reshape(9, -1)
    products = jnp.stack(
        [flat[6 + first] * flat[3 + second] for first in range(3) for second in range(3)], 0
    )
    onehot = (cell[:, None] == jnp.arange(count, dtype=jnp.int32)[None, :]).astype(jnp.float32)
    return (jnp.dot(products, onehot, precision=lax.Precision.HIGHEST), onehot)


def nodal_terms(sigma, data, node, owner, nodes):
    flat = data.reshape(9, -1)
    full = [
        [sigma[0], sigma[3], sigma[4]],
        [sigma[3], sigma[1], sigma[5]],
        [sigma[4], sigma[5], sigma[2]],
    ]
    burgers = flat[6:9]
    dline = flat[3:6]
    push = [
        full[row][0] * burgers[0] + full[row][1] * burgers[1] + full[row][2] * burgers[2]
        for row in range(3)
    ]
    force_x = push[1] * dline[2] - push[2] * dline[1]
    force_y = push[2] * dline[0] - push[0] * dline[2]
    force_z = push[0] * dline[1] - push[1] * dline[0]
    length = jnp.sqrt(dline[0] * dline[0] + dline[1] * dline[1] + dline[2] * dline[2])
    half = 0.5 * jnp.stack([force_x, force_y, force_z, length], 0)
    slot_start = owner[0] * nodes + node[0]
    slot_end = owner[1] * nodes + node[1]
    buffer = (
        jnp.zeros((4, 5 * nodes), jnp.float32).at[:, slot_start].add(half).at[:, slot_end].add(half)
    )
    return buffer.reshape(4, 5, nodes)


def on_device(
    offsets,
    line,
    burgers_kind,
    seg_cell,
    end_node,
    end_owner,
    drag,
    applied,
    pair_list,
    ghost_x_list,
    ghost_y_list,
):
    grid_x = lax.axis_size("gx")
    grid_y = lax.axis_size("gy")
    place_x = lax.axis_index("gx")
    place_y = lax.axis_index("gy")
    nodes = drag.shape[-1]
    count = CCX * CCY * NCZ
    cell = seg_cell[0, 0]
    data = segment_data(offsets[0, 0], line[0, 0], burgers_kind[0, 0], cell)
    blocks = data.shape[1]
    packet = pick_blocks(data, ghost_x_list[0, 0])
    beside_all = with_halo(packet, (("gx", 0),), 1)
    section = jnp.concatenate(
        [data, beside_all[0].at[0].add(-float(CCX)), beside_all[3].at[0].add(float(CCX))], axis=1
    )
    packet_y = pick_blocks(section, ghost_y_list[0, 0])
    around_y = with_halo(packet_y, (("gy", 0),), 1)
    ghosts = jnp.concatenate(
        [section, around_y[0].at[1].add(-float(CCY)), around_y[3].at[1].add(float(CCY))], axis=1
    )
    own_moments, onehot = cell_moments(data, cell, count)
    moments = lax.all_gather(own_moments[None], ("gx", "gy"), axis=0, tiled=True)
    far = far_stress(moments, place_x, place_y, grid_x, grid_y)
    pairs = pair_list[0, 0]
    real = jnp.sum((pairs[0] < blocks).astype(jnp.int32))
    turns = (real + pair_group - 1) // pair_group

    def body_step(index, total):
        targets = lax.dynamic_slice_in_dim(pairs[0], index * pair_group, pair_group)
        sources = lax.dynamic_slice_in_dim(pairs[1], index * pair_group, pair_group)
        piece = group_stress(data, ghosts, targets, sources)
        return total.at[:, targets].add(piece, mode="drop")

    near = lax.fori_loop(0, turns, body_step, jnp.zeros((6, blocks, data.shape[2]), jnp.float32))
    sigma = (
        near.reshape(6, -1)
        + jnp.dot(far, onehot.T, precision=lax.Precision.HIGHEST)
        + applied[:, None]
    )
    buffer = nodal_terms(sigma, data, end_node[0, 0], end_owner[0, 0], nodes)
    back_x = with_halo(jnp.stack([buffer[:, 1], buffer[:, 2]], 0), (("gx", 0),), 1)
    back_y = with_halo(jnp.stack([buffer[:, 3], buffer[:, 4]], 0), (("gy", 0),), 1)
    total = buffer[:, 0] + back_x[0] + back_x[3] + back_y[0] + back_y[3]
    velocity = total[0:3] / (drag[0, 0][None, :] * (total[3:4] + CORE_LENGTH))
    return velocity[None, None]


def solution(mesh):
    return jax.shard_map(
        on_device,
        mesh=mesh,
        in_specs=(
            P("gx", "gy", None, None),
            P("gx", "gy", None, None),
            P("gx", "gy", None),
            P("gx", "gy", None),
            P("gx", "gy", None, None),
            P("gx", "gy", None, None),
            P("gx", "gy", None),
            P(),
            P("gx", "gy", None, None),
            P("gx", "gy", None, None),
            P("gx", "gy", None, None),
        ),
        out_specs=P("gx", "gy", None, None),
        check_vma=False,
    )
```

profile of v0, /device:TPU:32, one launch (start us, length us, event | category | flops | bytes accessed | tf_op | source)
XLA Modules:
  0.0 1339.7 jit_solution(4860968595552354408)
XLA Ops:
  12.8 10.9 collective-permute-start.1
  26.8 348.0 %all-gather.1 = f32[256,9,64]{2,1,0:T(8,128)S(1)} all-gather(f32[1,9,64]{2,1,0:T(8,128)S(1)} %fusion.111), channel_id=2, replica_groups=mesh['gx'=32,'gy'=8] {'gx','gy'}, dimensions={0}, use_global_device_ids=true | all-gather | bytes 592128 | tf_op jit(solution)/shard_map/all_gather | solution.py:221
  375.3 82.1 %while.31 = (s32[]{:T(128)}, f32[6,64]{1,0:T(8,128)S(1)}, s32[16]{0:T(128)}, f32[256,9,64]{2,1,0:T(8,128)S(1)}, s32[]{:T(128)}, /*index=5*/s32[]{:T(128)}, s32[]...) while((s32[]{:T(128)}, f32[6,64]{1,0:T(8,128)S(1)}, ...), condition=%wide.region_17.18_spmd.clone.clone, body=%wide.region_10.17_spmd.clone.clone.sunk | while | flops 11415071 | bytes 295297 | solution.py:150
  461.8 6.2 collective-permute-start.3
  475.9 359.2 %while.30 = (s32[]{:T(128)}, f32[6,64,128]{2,0,1:T(8,128)S(1)}, s32[]{:T(128)}, s32[2,1024]{1,0:T(2,128)S(1)}, f32[9,64,128]{2,0,1:T(8,128)S(1)}, /*index=5*/f32...) while((s32[]{:T(128)}, f32[6,64,128]{2,0,1:T(8,128)S(1)}, s32[]{:T(128)}, ...), condition=%wide.region_9.10_spmd, body=%wide.region_1.9_spmd.sunk | while | flops 18364500 | bytes 635351 | solution.py:233
  477.3 3.4 fusion.199
  482.9 3.4 fusion.199
  494.1 3.4 fusion.199
  499.7 3.4 fusion.199
  510.9 3.4 fusion.199
  522.2 3.4 fusion.199
  527.8 3.4 fusion.199
  533.4 3.4 fusion.199
  539.0 3.4 fusion.199
  550.2 3.4 fusion.199
  555.8 3.4 fusion.199
  567.1 3.4 fusion.199
  572.7 3.4 fusion.199
  583.9 3.4 fusion.199
  589.5 3.4 fusion.199
  600.7 3.4 fusion.199
  606.3 3.4 fusion.199
  617.6 3.4 fusion.199
  623.2 3.4 fusion.199
  640.0 3.4 fusion.199
  645.6 3.4 fusion.199
  656.8 3.4 fusion.199
  662.5 3.4 fusion.199
  673.7 3.4 fusion.199
  690.5 3.4 fusion.199
  696.1 3.4 fusion.199
  707.4 3.4 fusion.199
  713.0 3.4 fusion.199
  718.6 3.4 fusion.199
  729.8 3.4 fusion.199
  741.0 3.4 fusion.199
  746.6 3.4 fusion.199
  752.3 3.4 fusion.199
  763.5 3.4 fusion.199
  769.1 3.4 fusion.199
  785.9 3.4 fusion.199
  791.5 3.4 fusion.199
  802.8 3.4 fusion.199
  839.1 52.6 %scatter_custom_fusion.1 = f32[4,40960]{0,1:T(8,128)} fusion(s32[8192]{0:T(1024)S(1)} %bitcast.349, f32[8192,4]{1,0:T(8,128)} %copy.143, f32[]{:T(128)} %constant.561.clone.1), kind=kCustom, calls=%fused_computation.221 | custom fusion | flops 32768 | bytes 655872 | tf_op jit(solution)/shard_map/scatter-add | solution.py:183
  891.7 53.8 %scatter_fusion.1 = f32[4,40960]{0,1:T(8,128)} fusion(f32[4,40960]{0,1:T(8,128)} %scatter_custom_fusion.1, s32[8192]{0:T(1024)S(1)} %bitcast.332, f32[8192,4]{1,0:T(8,128)} %copy.143), kind=kCustom, calls=%fused_computation.6 | custom fusion | flops 32768 | bytes 425984 | tf_op jit(solution)/shard_map/scatter-add | solution.py:183
  945.5 14.7 %fusion.180 = (f32[4,1,8192]{0,2,1:T(8,128)}, f32[4,1,8192]{0,2,1:T(8,128)}, f32[4,1,8192]{0,2,1:T(8,128)}, f32[4,1,8192]{0,2,1:T(8,128)}, f32[4,1,8192]{0,2,1:T(8,128)}) fusion(f32[4,5,8192]{0,2,1:T(8,128)} %bitcast.301), kind=kLoop, calls=%fused_computation.390 | loop fusion | bytes 1310720 | tf_op jit(solution)/shard_map/slice | solution.py:242
  971.8 171.1 %collective-permute-start.4 = (f32[1,4,8192]{2,1,0:T(4,128)S(1)}, f32[1,4,8192]{2,1,0:T(4,128)S(1)}, u32[]{:S(2)}, u32[]{:S(2)}) collective-permute-start(f32[1,4,8192]{2,1,0:T(4,128)S(1)} %bitcast.335), channel_id=1, source_target_pairs={{0,8},{8,16},{16,24},{24,32},{32,40},{40,48},{48,56},{56,64},{64,7... | collective-permute-start | bytes 393224 | tf_op jit(solution)/shard_map/ppermute | solution.py:30
  1147.9 190.9 %collective-permute-done.6 = f32[1,4,8192]{2,1,0:T(4,128)S(1)} collective-permute-done((f32[1,4,8192]{2,1,0:T(4,128)S(1)}, f32[1,4,8192]{2,1,0:T(4,128)S(1)}, u32[]{:S(2)}, u32[]{:S(2)}) %collective-permute-start.6) | collective-permute-done | bytes 131104 | tf_op jit(solution)/shard_map/ppermute | solution.py:30
  (1756 shorter events, 341.9 us)
Async XLA Ops:
  0.0 25.7 %copy-start.3 = (s32[1,1,8192]{2,1,0:T(1,128)S(1)}, s32[1,1,8192]{2,1,0:T(1,128)}, u32[]{:S(2)}) copy-start(s32[1,1,8192]{2,1,0:T(1,128)} %param.26) | copy-start | bytes 98308
  0.0 25.0 %copy-start = (f32[1,1,3,8192]{3,1,2,0:T(1,128)S(1)}, f32[1,1,3,8192]{3,1,2,0:T(1,128)}, u32[]{:S(2)}) copy-start(f32[1,1,3,8192]{3,1,2,0:T(1,128)} %param.24) | copy-start | bytes 294916
  12.0 446.4 %copy-start.1 = (s32[1,1,2,1024]{3,2,1,0:T(2,128)S(1)}, s32[1,1,2,1024]{3,2,1,0:T(2,128)}, u32[]{:S(2)}) copy-start(s32[1,1,2,1024]{3,2,1,0:T(2,128)} %param.31) | copy-start | bytes 24580
  12.8 447.8 %collective-permute-start.1 = (f32[1,9,32,128]{3,2,1,0:T(8,128)}, f32[1,9,32,128]{3,2,1,0:T(8,128)S(1)}, u32[]{:S(2)}, u32[]{:S(2)}) collective-permute-start(f32[1,9,32,128]{3,2,1,0:T(8,128)} %get-tuple-element.614), channel_id=1, source_target_pairs={{8,0},{16,8},{24,16},{32,24},{40,32},{48,40},{56,48},{64,56},{72,6... | collective-permute-start | bytes 442376 | tf_op jit(solution)/shard_map/ppermute | solution.py:32
  23.7 436.9 %collective-permute-start = (f32[1,9,32,128]{3,2,1,0:T(8,128)}, f32[1,9,32,128]{3,2,1,0:T(8,128)S(1)}, u32[]{:S(2)}, u32[]{:S(2)}) collective-permute-start(f32[1,9,32,128]{3,2,1,0:T(8,128)} %get-tuple-element.615), channel_id=1, source_target_pairs={{0,8},{8,16},{16,24},{24,32},{32,40},{40,48},{48,56},{56,64},{64,7... | collective-permute-start | bytes 442376 | tf_op jit(solution)/shard_map/ppermute | solution.py:30
  461.8 8.9 collective-permute-start.3
  468.0 4.8 collective-permute-start.2
  470.7 364.4 %copy-start.4 = (f32[6]{0:T(128)S(1)}, f32[6]{0:T(128)}, u32[]{:S(2)}) copy-start(f32[6]{0:T(128)} %param.30) | copy-start | bytes 76
  968.7 370.1 %copy-start.2 = (f32[1,1,8192]{2,1,0:T(1,128)S(1)}, f32[1,1,8192]{2,1,0:T(1,128)}, u32[]{:S(2)}) copy-start(f32[1,1,8192]{2,1,0:T(1,128)} %param.29) | copy-start | bytes 98308
  971.6 174.2 %collective-permute-start.7 = (f32[1,4,8192]{2,1,0:T(4,128)S(1)}, f32[1,4,8192]{2,1,0:T(4,128)S(1)}, u32[]{:S(2)}, u32[]{:S(2)}) collective-permute-start(f32[1,4,8192]{2,1,0:T(4,128)S(1)} %bitcast.336), channel_id=1, source_target_pairs={{1,0},{2,1},{3,2},{4,3},{5,4},{6,5},{7,6},{0,7},{9,8},{10,9},{11,1... | collective-permute-start | bytes 393224 | tf_op jit(solution)/shard_map/ppermute | solution.py:32
  971.8 173.9 %collective-permute-start.4 = (f32[1,4,8192]{2,1,0:T(4,128)S(1)}, f32[1,4,8192]{2,1,0:T(4,128)S(1)}, u32[]{:S(2)}, u32[]{:S(2)}) collective-permute-start(f32[1,4,8192]{2,1,0:T(4,128)S(1)} %bitcast.335), channel_id=1, source_target_pairs={{0,8},{8,16},{16,24},{24,32},{32,40},{40,48},{48,56},{56,64},{64,7... | collective-permute-start | bytes 393224 | tf_op jit(solution)/shard_map/ppermute | solution.py:30
  1142.9 5.0 collective-permute-start.5
  1142.9 195.9 %collective-permute-start.6 = (f32[1,4,8192]{2,1,0:T(4,128)S(1)}, f32[1,4,8192]{2,1,0:T(4,128)S(1)}, u32[]{:S(2)}, u32[]{:S(2)}) collective-permute-start(f32[1,4,8192]{2,1,0:T(4,128)S(1)} %bitcast.333), channel_id=1, source_target_pairs={{0,1},{1,2},{2,3},{3,4},{4,5},{5,6},{6,7},{7,0},{8,9},{9,10},{10,1... | collective-permute-start | bytes 393224 | tf_op jit(solution)/shard_map/ppermute | solution.py:30
where the time goes:
time: 1350 us; the launch traced here: 1340 us
  other arithmetic  430 us (32%)
  blocking collectives  348 us (26%)
  waiting for transfers between devices  196 us (15%)
  starting transfers between devices  188 us (14%)
  local copies, waits for them, and re-layouts  153 us (11%)
  loops' own time  20.7 us (2%)
    all_gather x1, blocking collectives, on_device(): lax.all_gather(own_moments[None], ('gx', 'gy'), axis=0, tiled=True)  348 us
    reduce_sum x64, other arithmetic, group_stress(): return jnp.stack([jnp.sum(piece, axis=-1) for piece in parts], 0)  216 us
    ppermute x4, waiting for transfers between devices, with_halo(): lax.ppermute(tail, axis, [(i, (i + 1) % count) for i in range(count)])  193 us
    ppermute x4, starting transfers between devices, with_halo(): lax.ppermute(tail, axis, [(i, (i + 1) % count) for i in range(count)])  171 us
    scatter-add x2, other arithmetic, nodal_terms(): jnp.zeros((4, 5 * nodes), jnp.float32).at[:, slot_start].add(half)  106 us
    scatter-add x64, other arithmetic, body_step(): return total.at[:, targets].add(piece, mode='drop')  49.8 us
    gather x64, local copies, waits for them, and re-layouts, group_stress(): target_data = owned[:, jnp.clip(targets, 0, blocks - 1)]  35.5 us
    gather x64, local copies, waits for them, and re-layouts, group_stress(): source_data = ghosts[:, sources]  35.5 us
  transfers between devices with their start and end apart: 8, of which 4 were waited for; matrix products, arithmetic and copies ran while one was open for 6% of the time, Pallas kernels for 0%

commit v1 on v0

v1 whole, which is shorter than its diff:
```python
import functools
import math

import jax
import jax.numpy as jnp
from jax import lax
from jax.experimental import pallas as pl
from jax.experimental.pallas import tpu as pltpu
from jax.sharding import PartitionSpec as P

SEG = 128
CCX = 1
CCY = 4
NCZ = 16
CORE_SQUARE = 0.25
SHEAR_TERM = 1.0 / (8.0 * math.pi)
BULK_TERM = 1.0 / (4.0 * math.pi * 0.7)
CORE_LENGTH = 1.0
COMPONENTS = ((0, 0), (1, 1), (2, 2), (0, 1), (0, 2), (1, 2))
CUBICS = (
    ((1.0, 0, (0, 0, 0)), (1.0, 1, (1, 0, 0)), (1.0, 2, (2, 0, 0))),
    ((1.0, 0, (0, 1, 1)), (1.0, 1, (1, 1, 1)), (1.0, 2, (2, 1, 1))),
    (
        (-1.0, 0, (0, 0, 0)),
        (-1.0, 1, (1, 0, 0)),
        (-1.0, 2, (2, 0, 0)),
        (-1.0, 0, (0, 1, 1)),
        (-1.0, 1, (1, 1, 1)),
        (-1.0, 2, (2, 1, 1)),
    ),
    ((1.0, 0, (0, 0, 1)), (1.0, 1, (1, 0, 1)), (1.0, 2, (2, 0, 1))),
    ((1.0, 0, (0, 0, 2)), (1.0, 1, (0, 1, 2)), (-1.0, 2, (0, 0, 0)), (-1.0, 2, (0, 1, 1))),
    ((1.0, 0, (0, 1, 2)), (1.0, 1, (1, 1, 2)), (-1.0, 2, (0, 0, 1)), (-1.0, 2, (1, 1, 1))),
)
CENTER = (CCX / 2.0, CCY / 2.0, NCZ / 2.0)
UNROLL = 4
TRANSPOSED = (((1,), (1,)), ((), ()))
f32 = jnp.float32
bf16 = jnp.bfloat16


def burgers_of(kind):
    code = kind.astype(jnp.int32)
    return [1.0 - 2.0 * ((code >> bit) & 1).astype(f32) for bit in range(3)]


def source_columns(place, dline, kind):
    burgers = burgers_of(kind)
    amat = [[burgers[i] * dline[j] for j in range(3)] for i in range(3)]
    curl = [
        amat[1][2] - amat[2][1],
        amat[2][0] - amat[0][2],
        amat[0][1] - amat[1][0],
    ]
    turned = {
        (0, 0): (None, 2.0 * amat[2][0], -2.0 * amat[1][0]),
        (1, 1): (-2.0 * amat[2][1], None, 2.0 * amat[0][1]),
        (2, 2): (2.0 * amat[1][2], -2.0 * amat[0][2], None),
        (0, 1): (-amat[2][0], amat[2][1], amat[0][0] - amat[1][1]),
        (0, 2): (amat[1][0], amat[2][2] - amat[0][0], -amat[1][2]),
        (1, 2): (amat[1][1] - amat[2][2], -amat[0][1], amat[0][2]),
    }
    bulk3 = 3.0 * BULK_TERM
    curl_k = [BULK_TERM * item for item in curl]
    curl_3k = [bulk3 * item for item in curl]
    pairs = {(a, b): place[a] * place[b] for a in range(3) for b in range(a, 3)}
    single = [[curl_3k[i] * place[a] for a in range(3)] for i in range(3)]
    double = {}

    def doubled(i, a, b):
        key = (i, min(a, b), max(a, b))
        if key not in double:
            double[key] = curl_3k[i] * pairs[key[1:]]
        return double[key]

    columns = []
    for comp, (a, b) in enumerate(COMPONENTS):
        linear5 = [0.0, 0.0, 0.0]
        linear3 = [0.0, 0.0, 0.0]
        const5 = 0.0
        for sign, i, axes in CUBICS[comp]:
            for spot in range(3):
                rest = axes[:spot] + axes[spot + 1 :]
                linear5[axes[spot]] = linear5[axes[spot]] - sign * doubled(i, *rest)
            const5 = const5 + sign * (doubled(i, axes[0], axes[1]) * place[axes[2]])
        for axis in range(3):
            alpha3 = 0.0
            alpha5 = 0.0
            if turned[(a, b)][axis] is not None:
                alpha3 = (2.0 * SHEAR_TERM) * turned[(a, b)][axis]
                alpha5 = (3.0 * CORE_SQUARE * SHEAR_TERM) * turned[(a, b)][axis]
            if axis == b:
                alpha3 = alpha3 + curl_k[a]
            if axis == a:
                alpha3 = alpha3 + curl_k[b]
            if a == b:
                alpha3 = alpha3 - curl_k[axis]
                alpha5 = alpha5 - (3.0 * CORE_SQUARE) * curl_k[axis]
            if (a, b) == (2, 2):
                alpha3 = alpha3 - curl_3k[axis]
                alpha5 = alpha5 + CORE_SQUARE * curl_3k[axis]
            if b == 2 and a == axis and a < 2:
                alpha3 = alpha3 - curl_3k[2]
                alpha5 = alpha5 + CORE_SQUARE * curl_3k[2]
            linear3[axis] = alpha3
            linear5[axis] = linear5[axis] + alpha5
            const5 = const5 - alpha5 * place[axis]
        const3 = -(linear3[0] * place[0] + linear3[1] * place[1] + linear3[2] * place[2])
        columns.append((comp, const3, const5))
        for axis in range(3):
            columns.append((8 * (axis + 1) + comp, linear3[axis], linear5[axis]))
    spots = (32, 33, 34, 35, 36, 37, 38, 39, 6)
    for i in range(3):
        for a in range(3):
            columns.append((spots[3 * i + a], None, single[i][a]))
        columns.append((8 * (i + 1) + 6, None, curl_3k[i]))
    return columns


def parts_of(value):
    head = value.astype(bf16).astype(f32)
    rest = value - head
    middle = rest.astype(bf16).astype(f32)
    return head, middle, rest - middle


def near_kernel(
    blocks, ghosts, count_ref, pairs_ref, gh_ref, base_ref, out_ref, xb, qt, acc, scr3, scr5
):
    zero = jnp.zeros((SEG, SEG), f32)
    for part in range(8):
        scr3[pl.ds(part * SEG, SEG), :] = zero
        scr5[pl.ds(part * SEG, SEG), :] = zero

    def source_step(group, carry):
        first = pl.multiple_of(group * 64, 64)
        rows = [gh_ref[pl.ds(first + row, 8, stride=8), :] for row in range(7)]
        for spot, term3, term5 in source_columns(rows[0:3], rows[3:6], rows[6]):
            for shift, piece in zip((0, 40, 80), parts_of(term5)):
                scr5[pl.ds(spot + shift, 8, stride=SEG), :] = piece
            if term3 is not None:
                for shift, piece in zip((0, 40, 80), parts_of(term3)):
                    scr3[pl.ds(spot + shift, 8, stride=SEG), :] = piece
        for part in range(8):
            qt[group * 8 + part, :, 0:SEG] = scr3[pl.ds(part * SEG, SEG), :].astype(bf16)
            qt[group * 8 + part, :, SEG : 2 * SEG] = scr5[pl.ds(part * SEG, SEG), :].astype(bf16)
        return carry

    lax.fori_loop(0, ghosts // 8, source_step, 0)

    def target_step(block, carry):
        tile = gh_ref[pl.ds(pl.multiple_of(block * 8, 8), 8), :]
        columns = jnp.transpose(tile)
        for axis in range(3):
            xb[3 * block + axis] = jnp.broadcast_to(columns[:, axis : axis + 1], (SEG, SEG))
        acc[block] = zero
        return carry

    lax.fori_loop(0, blocks, target_step, 0)

    def pair_step(turn, carry):
        for part in range(UNROLL):
            target = pairs_ref[0, turn * UNROLL + part]
            source = pairs_ref[1, turn * UNROLL + part]
            tile = gh_ref[pl.ds(pl.multiple_of(source * 8, 8), 8), :]
            heads = []
            tails = []
            for first in range(0, SEG, 32):
                dx = xb[3 * target, first : first + 32, :] - tile[0:1]
                dy = xb[3 * target + 1, first : first + 32, :] - tile[1:2]
                dz = xb[3 * target + 2, first : first + 32, :] - tile[2:3]
                inv_one = lax.rsqrt((dx * dx + CORE_SQUARE) + dy * dy + dz * dz)
                inv_two = inv_one * inv_one
                inv_three = inv_two * inv_one
                inv_five = inv_three * inv_two
                head3 = inv_three.astype(bf16)
                head5 = inv_five.astype(bf16)
                heads.append(jnp.concatenate([head3, head5], axis=1))
                tails.append(
                    jnp.concatenate(
                        [
                            (inv_three - head3.astype(f32)).astype(bf16),
                            (inv_five - head5.astype(f32)).astype(bf16),
                        ],
                        axis=1,
                    )
                )
            weight = qt[source]
            piece = lax.dot_general(
                jnp.concatenate(heads, axis=0), weight, TRANSPOSED, preferred_element_type=f32
            ) + lax.dot_general(
                jnp.concatenate(tails, axis=0), weight, TRANSPOSED, preferred_element_type=f32
            )
            acc[target] = acc[target] + piece
        return carry

    lax.fori_loop(0, count_ref[0] // UNROLL, pair_step, 0)

    def force_step(block, carry):
        first = pl.multiple_of(block * 8, 8)
        tile = gh_ref[pl.ds(first, 8), :]
        sums = jnp.transpose(acc[block])
        sums = sums[0:40] + sums[40:80] + sums[80:120]
        place = [tile[axis : axis + 1] for axis in range(3)]
        dline = [tile[3 + axis : 4 + axis] for axis in range(3)]
        burgers = burgers_of(tile[6:7])
        linear = base_ref[:, pl.ds(pl.multiple_of(block * SEG, SEG), SEG)] + (
            sums[0:8] + place[0] * sums[8:16] + place[1] * sums[16:24] + place[2] * sums[24:32]
        )
        outer = [sums[32 + item : 33 + item] for item in range(8)] + [sums[6:7]]
        lone = [sums[14:15], sums[22:23], sums[30:31]]
        twice = {(a, b): place[a] * place[b] for a in range(3) for b in range(a, 3)}
        sigma = []
        for comp in range(6):
            total = linear[comp : comp + 1]
            if comp != 2:
                curved = 0.0
                for sign, i, axes in CUBICS[comp]:
                    value = lone[i] * place[axes[2]] - outer[3 * i + axes[2]]
                    value = value * twice[tuple(sorted(axes[:2]))]
                    value = value - place[axes[2]] * (
                        outer[3 * i + axes[0]] * place[axes[1]]
                        + outer[3 * i + axes[1]] * place[axes[0]]
                    )
                    curved = curved + sign * value
                sigma.append((total, curved))
            else:
                sigma.append((total, -(sigma[0][1] + sigma[1][1])))
        sigma = [total - curved for total, curved in sigma]
        full = [
            [sigma[0], sigma[3], sigma[4]],
            [sigma[3], sigma[1], sigma[5]],
            [sigma[4], sigma[5], sigma[2]],
        ]
        push = [
            full[row][0] * burgers[0] + full[row][1] * burgers[1] + full[row][2] * burgers[2]
            for row in range(3)
        ]
        force = [
            push[1] * dline[2] - push[2] * dline[1],
            push[2] * dline[0] - push[0] * dline[2],
            push[0] * dline[1] - push[1] * dline[0],
        ]
        length = jnp.sqrt(dline[0] * dline[0] + dline[1] * dline[1] + dline[2] * dline[2])
        out_ref[pl.ds(first, 8), :] = 0.5 * jnp.concatenate(
            force + [length] + sigma[0:4], axis=0
        )
        return carry

    lax.fori_loop(0, blocks, force_step, 0)


def near_call(count, pairs, ghosts, base):
    blocks = base.shape[1] // SEG
    number = ghosts.shape[0] // 8
    return pl.pallas_call(
        functools.partial(near_kernel, blocks, number),
        out_shape=jax.ShapeDtypeStruct((blocks * 8, SEG), f32),
        in_specs=[
            pl.BlockSpec(memory_space=pltpu.SMEM),
            pl.BlockSpec(memory_space=pltpu.SMEM),
            pl.BlockSpec(memory_space=pltpu.VMEM),
            pl.BlockSpec(memory_space=pltpu.VMEM),
        ],
        out_specs=pl.BlockSpec(memory_space=pltpu.VMEM),
        scratch_shapes=[
            pltpu.VMEM((3 * blocks, SEG, SEG), f32),
            pltpu.VMEM((number, SEG, 2 * SEG), bf16),
            pltpu.VMEM((blocks, SEG, SEG), f32),
            pltpu.VMEM((8 * SEG, SEG), f32),
            pltpu.VMEM((8 * SEG, SEG), f32),
        ],
        compiler_params=pltpu.CompilerParams(vmem_limit_bytes=48 * 1024 * 1024),
    )(count, pairs, ghosts, base)


def wrapped(diff, extent):
    half = extent / 2.0
    return jnp.where(diff > half, diff - extent, jnp.where(diff < -half, diff + extent, diff))


def far_rows(plus, minus, step):
    both = [[plus[3 * i + j] + minus[3 * i + j] for j in range(3)] for i in range(3)]
    odd = [[plus[3 * i + j] - minus[3 * i + j] for j in range(3)] for i in range(3)]

    def curl_of(amat):
        return (amat[1][2] - amat[2][1], amat[2][0] - amat[0][2], amat[0][1] - amat[1][0])

    curl_both = curl_of(both)
    curl_odd = curl_of(odd)
    shear = SHEAR_TERM
    turned = [
        (None, 2.0 * both[2][0], -2.0 * both[1][0]),
        (step * (-2.0 * odd[2][1]), None, 2.0 * both[0][1]),
        (step * (2.0 * odd[1][2]), -2.0 * both[0][2], None),
        (step * -odd[2][0], both[2][1], both[0][0] - both[1][1]),
        (step * odd[1][0], both[2][2] - both[0][0], -both[1][2]),
        (step * (odd[1][1] - odd[2][2]), -both[0][1], both[0][2]),
    ]
    turned = [[None if item is None else shear * item for item in line] for line in turned]
    curls = {
        "ox": BULK_TERM * step * curl_odd[0],
        "oy": BULK_TERM * step * curl_odd[1],
        "oz": BULK_TERM * step * curl_odd[2],
        "bx": BULK_TERM * curl_both[0],
        "by": BULK_TERM * curl_both[1],
        "bz": BULK_TERM * curl_both[2],
        "sx": BULK_TERM * step * step * curl_both[0],
    }
    return turned, curls


def exchange_kernel(
    nx,
    ny,
    off_ref,
    line_ref,
    kind_ref,
    cell_ref,
    applied_ref,
    listx_ref,
    listy_ref,
    gh_ref,
    base_ref,
    products,
    hot,
    pack_x,
    land_x,
    pack_y,
    land_y,
    mine,
    row_land,
    row_block,
    all_land,
    far_acc,
    sem_x,
    sem_y,
    row_send,
    row_recv,
    all_send,
    all_recv,
):
    segs = off_ref.shape[1]
    blocks = segs // SEG
    packet = listx_ref.shape[1]
    cells = hot.shape[0]
    me_x = lax.axis_index("gx")
    me_y = lax.axis_index("gy")
    mesh_ids = pl.DeviceIdType.MESH
    barrier = pltpu.get_barrier_semaphore()

    def greet_x(step, carry):
        pl.semaphore_signal(
            barrier, inc=1, device_id=(lax.rem(me_x + step, nx), me_y), device_id_type=mesh_ids
        )
        return carry

    def greet_y(step, carry):
        pl.semaphore_signal(
            barrier, inc=1, device_id=(me_x, lax.rem(me_y + step, ny)), device_id_type=mesh_ids
        )
        return carry

    lax.fori_loop(1, nx, greet_x, 0)
    lax.fori_loop(1, ny, greet_y, 0)

    cell_iota = lax.broadcasted_iota(jnp.int32, (cells, SEG), 0)
    origin = [0.5 - CENTER[axis] for axis in range(3)]

    def block_step(block, carry):
        lanes = pl.ds(pl.multiple_of(block * SEG, SEG), SEG)
        cell = cell_ref[:, lanes]
        kind = kind_ref[:, lanes]
        dline = line_ref[:, lanes]
        shift = off_ref[:, lanes]
        corner = (cell // (CCY * NCZ), cell // NCZ % CCY, cell % NCZ)
        place = [
            (corner[axis].astype(f32) + origin[axis]) + shift[axis : axis + 1] for axis in range(3)
        ]
        code = kind.astype(f32)
        gh_ref[block] = jnp.concatenate(
            place + [dline, code, jnp.zeros((1, SEG), f32)], axis=0
        )
        burgers = burgers_of(code)
        outer = jnp.concatenate(
            [burgers[0] * dline, burgers[1] * dline, burgers[2] * dline, jnp.zeros((7, SEG), f32)],
            axis=0,
        )
        for part, piece in enumerate(parts_of(outer)):
            products[part * 16 : part * 16 + 16, lanes] = piece.astype(bf16)
        hot[:, lanes] = (cell_iota == cell).astype(f32).astype(bf16)
        return carry

    lax.fori_loop(0, blocks, block_step, 0)

    def pick_x(item, carry):
        for side in range(2):
            source = listx_ref[side, item]
            pack_x[side, item] = gh_ref[source]
        return carry

    lax.fori_loop(0, packet, pick_x, 0)
    pl.semaphore_wait(barrier, nx - 1 + ny - 1)

    copies_x = []
    for side in range(2):
        target = lax.rem(me_x + (nx - 1 if side == 0 else 1), nx)
        copies_x.append(
            pltpu.make_async_remote_copy(
                src_ref=pack_x.at[side],
                dst_ref=land_x.at[1 - side],
                send_sem=sem_x.at[side],
                recv_sem=sem_x.at[2 + side],
                device_id=(target, me_y),
                device_id_type=mesh_ids,
            )
        )
    for copy in copies_x:
        copy.start()

    moments = lax.dot_general(products[...], hot[...], TRANSPOSED, preferred_element_type=f32)
    moments = moments[0:16] + moments[16:32] + moments[32:48]
    mine[...] = jnp.concatenate([moments, jnp.zeros((16, SEG - cells), f32)], axis=1)
    row_land[me_y] = mine[...]

    def row_copy(step):
        return pltpu.make_async_remote_copy(
            src_ref=mine,
            dst_ref=row_land.at[me_y],
            send_sem=row_send.at[step],
            recv_sem=row_recv.at[step],
            device_id=(me_x, lax.rem(me_y + step, ny)),
            device_id_type=mesh_ids,
        )

    def row_start(step, carry):
        row_copy(step).start()
        return carry

    def row_wait(step, carry):
        row_copy(step).wait()
        return carry

    lax.fori_loop(1, ny, row_start, 0)

    row_iota = lax.broadcasted_iota(jnp.int32, (8, SEG), 0)
    for copy in copies_x:
        copy.wait()
    for slot in range(2):
        moved = jnp.where(row_iota == 0, -float(CCX) if slot == 0 else float(CCX), 0.0)

        def take_x(item, carry, slot=slot, moved=moved):
            gh_ref[blocks + slot * packet + item] = land_x[slot, item] + moved
            return carry

        lax.fori_loop(0, packet, take_x, 0)

    def pick_y(item, carry):
        for side in range(2):
            source = listy_ref[side, item]
            pack_y[side, item] = gh_ref[source]
        return carry

    lax.fori_loop(0, packet, pick_y, 0)
    copies_y = []
    for side in range(2):
        target = lax.rem(me_y + (ny - 1 if side == 0 else 1), ny)
        copies_y.append(
            pltpu.make_async_remote_copy(
                src_ref=pack_y.at[side],
                dst_ref=land_y.at[1 - side],
                send_sem=sem_y.at[side],
                recv_sem=sem_y.at[2 + side],
                device_id=(me_x, target),
                device_id_type=mesh_ids,
            )
        )
    for copy in copies_y:
        copy.start()

    lax.fori_loop(1, ny, row_wait, 0)
    lane_iota = lax.broadcasted_iota(jnp.int32, (16, SEG), 1)
    lasts = []
    for tile in range(4):
        first = row_land[2 * tile]
        second = row_land[2 * tile + 1]
        merged = jnp.where(lane_iota < cells, first, pltpu.roll(second, cells, 1))
        row_block[8 * tile : 8 * tile + 8, :] = merged[0:8]
        lasts.append(merged[8:9])
    row_block[32:40, :] = jnp.concatenate(lasts + [jnp.zeros((4, SEG), f32)], axis=0)
    all_land[me_x] = row_block[...]

    def all_copy(step):
        return pltpu.make_async_remote_copy(
            src_ref=row_block,
            dst_ref=all_land.at[me_x],
            send_sem=all_send.at[step],
            recv_sem=all_recv.at[step],
            device_id=(lax.rem(me_x + step, nx), me_y),
            device_id_type=mesh_ids,
        )

    def all_start(step, carry):
        all_copy(step).start()
        return carry

    def all_wait(step, carry):
        all_copy(step).wait()
        return carry

    lax.fori_loop(1, nx, all_start, 0)

    for copy in copies_y:
        copy.wait()
    for slot in range(2):
        moved = jnp.where(row_iota == 1, -float(CCY) if slot == 0 else float(CCY), 0.0)

        def take_y(item, carry, slot=slot, moved=moved):
            gh_ref[blocks + (2 + slot) * packet + item] = land_y[slot, item] + moved
            return carry

        lax.fori_loop(0, packet, take_y, 0)

    far_acc[...] = jnp.zeros_like(far_acc)
    lax.fori_loop(1, nx, all_wait, 0)

    lane = lax.broadcasted_iota(jnp.int32, (8, SEG), 1)
    source_z = (lane % NCZ).astype(f32)
    depth = [
        wrapped((row_iota + 8 * half).astype(f32) - source_z, float(NCZ)) for half in range(2)
    ]
    extent_y = float(CCY * ny)

    def far_step(turn, carry):
        apart = turn // 4
        tile = turn % 4
        step = apart.astype(f32)
        middle = apart == nx // 2
        upper = me_x >= nx // 2
        weight_plus = jnp.where(middle & jnp.logical_not(upper), 0.0, 1.0)
        weight_minus = jnp.where((apart == 0) | (middle & upper), 0.0, 1.0)
        place_plus = lax.rem(me_x - apart + nx, nx)
        place_minus = lax.rem(me_x + apart, nx)
        rows = pl.ds(pl.multiple_of(tile * 8, 8), 8)
        head_plus = all_land[place_plus, rows, :] * weight_plus
        head_minus = all_land[place_minus, rows, :] * weight_minus
        plus = [head_plus[item : item + 1] for item in range(8)]
        minus = [head_minus[item : item + 1] for item in range(8)]
        plus.append(all_land[place_plus, pl.ds(32 + tile, 1), :] * weight_plus)
        minus.append(all_land[place_minus, pl.ds(32 + tile, 1), :] * weight_minus)
        turned, curls = far_rows(plus, minus, step)
        source_y = (lane // NCZ + tile * 8).astype(f32)
        close = apart <= 1
        for quarter in range(CCY):
            ry = wrapped((me_y * CCY + quarter).astype(f32) - source_y, extent_y)
            plane = (ry * ry + CORE_SQUARE) + step * step
            beside = jnp.logical_and(jnp.abs(ry) <= 1.0, close)
            for half in range(2):
                rz = depth[half]
                inv_one = lax.rsqrt(plane + rz * rz)
                keep = jnp.logical_and(beside, jnp.abs(rz) <= 1.0)
                inv_two = inv_one * inv_one
                inv_three = jnp.where(keep, 0.0, inv_two * inv_one)
                inv_five = inv_three * inv_two
                gain = 2.0 * inv_three + (3.0 * CORE_SQUARE) * inv_five
                dot_both = curls["ox"] + ry * curls["by"] + rz * curls["bz"]
                dot_odd = curls["sx"] + ry * curls["oy"] + rz * curls["oz"]
                trace = (inv_three + (3.0 * CORE_SQUARE) * inv_five) * dot_both
                thrice = 3.0 * inv_five
                wave = thrice * dot_both
                wave_odd = thrice * dot_odd
                wave_y = wave * ry
                bends = (
                    2.0 * curls["ox"],
                    2.0 * (ry * curls["by"]),
                    2.0 * (rz * curls["bz"]),
                    ry * curls["bx"] + curls["oy"],
                    rz * curls["bx"] + curls["oz"],
                    rz * curls["by"] + ry * curls["bz"],
                )
                curved = (
                    wave * (step * step),
                    wave_y * ry,
                    (wave * rz) * rz,
                    wave_odd * ry,
                    wave_odd * rz,
                    wave_y * rz,
                )
                spot = 8 * (2 * quarter + half)
                for comp in range(6):
                    swirl = None
                    for factor, item in zip((None, ry, rz), turned[comp]):
                        if item is not None:
                            item = item if factor is None else factor * item
                            swirl = item if swirl is None else swirl + item
                    value = gain * swirl + inv_three * bends[comp] - curved[comp]
                    if comp < 3:
                        value = value - trace
                    far_acc[comp, spot : spot + 8, :] = far_acc[comp, spot : spot + 8, :] + value
        return carry

    lax.fori_loop(0, 4 * (nx // 2 + 1), far_step, 0)

    pick = (
        lax.broadcasted_iota(jnp.int32, (8, 6 * SEG), 1) // SEG
        == lax.broadcasted_iota(jnp.int32, (8, 6 * SEG), 0)
    ).astype(f32)
    far = lax.dot_general(
        pick,
        jnp.concatenate([far_acc[comp] for comp in range(6)], axis=1),
        TRANSPOSED,
        precision=lax.Precision.HIGHEST,
        preferred_element_type=f32,
    )
    far = jnp.concatenate(list(parts_of(far)) + [jnp.zeros((8, cells), f32)], axis=0).astype(bf16)
    outside = jnp.zeros((8, 1), f32)
    comp_iota = lax.broadcasted_iota(jnp.int32, (8, 1), 0)
    for comp in range(6):
        outside = jnp.where(comp_iota == comp, applied_ref[comp], outside)
    width = 8 * SEG

    def base_step(part, carry):
        lanes = pl.ds(pl.multiple_of(part * width, width), width)
        value = jnp.dot(far, hot[:, lanes], preferred_element_type=f32)
        base_ref[:, lanes] = (value[0:8] + value[8:16] + value[16:24]) + outside
        return carry

    lax.fori_loop(0, segs // width, base_step, 0)


def exchange_call(nx, ny, offsets, dline, kind, cell, applied, list_x, list_y):
    segs = offsets.shape[1]
    blocks = segs // SEG
    packet = list_x.shape[1]
    number = blocks + 4 * packet
    cells = CCX * CCY * NCZ
    vmem = pl.BlockSpec(memory_space=pltpu.VMEM)
    smem = pl.BlockSpec(memory_space=pltpu.SMEM)
    return pl.pallas_call(
        functools.partial(exchange_kernel, nx, ny),
        out_shape=(
            jax.ShapeDtypeStruct((number, 8, SEG), f32),
            jax.ShapeDtypeStruct((8, segs), f32),
        ),
        in_specs=[vmem] * 4 + [smem] * 3,
        out_specs=(vmem, vmem),
        scratch_shapes=[
            pltpu.VMEM((48, segs), bf16),
            pltpu.VMEM((cells, segs), bf16),
            pltpu.VMEM((2, packet, 8, SEG), f32),
            pltpu.VMEM((2, packet, 8, SEG), f32),
            pltpu.VMEM((2, packet, 8, SEG), f32),
            pltpu.VMEM((2, packet, 8, SEG), f32),
            pltpu.VMEM((16, SEG), f32),
            pltpu.VMEM((ny, 16, SEG), f32),
            pltpu.VMEM((40, SEG), f32),
            pltpu.VMEM((nx, 40, SEG), f32),
            pltpu.VMEM((6, cells, SEG), f32),
            pltpu.SemaphoreType.DMA((4,)),
            pltpu.SemaphoreType.DMA((4,)),
            pltpu.SemaphoreType.DMA((ny,)),
            pltpu.SemaphoreType.DMA((ny,)),
            pltpu.SemaphoreType.DMA((nx,)),
            pltpu.SemaphoreType.DMA((nx,)),
        ],
        compiler_params=pltpu.CompilerParams(
            collective_id=0, has_side_effects=True, vmem_limit_bytes=32 * 1024 * 1024
        ),
    )(offsets, dline, kind, cell, applied, list_x, list_y)


NODE_COLS = 256
CHUNK = 2048


def nodal_kernel(
    nx,
    ny,
    half_ref,
    node_ref,
    owner_ref,
    drag_ref,
    out_ref,
    column_hot,
    row_hot,
    totals,
    outgoing,
    landing,
    send_sem,
    recv_sem,
):
    segs = node_ref.shape[1]
    rows = drag_ref.shape[0]
    me_x = lax.axis_index("gx")
    me_y = lax.axis_index("gy")
    mesh_ids = pl.DeviceIdType.MESH
    beside = (
        (lax.rem(me_x + nx - 1, nx), me_y),
        (lax.rem(me_x + 1, nx), me_y),
        (me_x, lax.rem(me_y + ny - 1, ny)),
        (me_x, lax.rem(me_y + 1, ny)),
    )
    barrier = pltpu.get_barrier_semaphore()
    for device in beside:
        pl.semaphore_signal(barrier, inc=1, device_id=device, device_id_type=mesh_ids)

    column_iota = lax.broadcasted_iota(jnp.int32, (NODE_COLS, SEG), 0)

    def column_step(block, carry):
        lanes = pl.ds(pl.multiple_of(block * SEG, SEG), SEG)
        for end in range(2):
            column = node_ref[end : end + 1, lanes] % NODE_COLS
            where = pl.ds(pl.multiple_of(end * segs + block * SEG, SEG), SEG)
            column_hot[:, where] = (column_iota == column).astype(f32).astype(bf16)
        return carry

    lax.fori_loop(0, segs // SEG, column_step, 0)

    def add_up(first_row, count):
        row_iota = lax.broadcasted_iota(jnp.int32, (count, SEG), 0) + first_row

        def chunk_step(chunk, carry):
            for end in range(2):

                def tile_step(tile, inner):
                    block = chunk * (CHUNK // SEG) + tile
                    lanes = pl.ds(pl.multiple_of(block * SEG, SEG), SEG)
                    slot = (
                        owner_ref[end : end + 1, lanes] * rows
                        + node_ref[end : end + 1, lanes] // NODE_COLS
                    )
                    mask = row_iota == slot
                    values = half_ref[pl.ds(pl.multiple_of(block * 8, 8), 8), :]
                    heads = values.astype(bf16).astype(f32)
                    tails = values - heads
                    where = pl.ds(pl.multiple_of(tile * SEG, SEG), SEG)
                    for item in range(4):
                        for part, piece in enumerate((heads, tails)):
                            spot = (2 * item + part) * count
                            row_hot[spot : spot + count, where] = jnp.where(
                                mask, piece[item : item + 1], 0.0
                            ).astype(bf16)
                    return inner

                lax.fori_loop(0, CHUNK // SEG, tile_step, 0)
                where = pl.ds(pl.multiple_of(end * segs + chunk * CHUNK, CHUNK), CHUNK)
                totals[0 : 8 * count, :] = totals[0 : 8 * count, :] + lax.dot_general(
                    row_hot[0 : 8 * count, :],
                    column_hot[:, where],
                    TRANSPOSED,
                    preferred_element_type=f32,
                )
            return carry

        totals[0 : 8 * count, :] = jnp.zeros((8 * count, NODE_COLS), f32)
        lax.fori_loop(0, segs // CHUNK, chunk_step, 0)

    add_up(rows, 4 * rows)
    for side in range(4):
        for item in range(4):
            spot = 2 * item * 4 * rows + side * rows
            outgoing[side, item * rows : (item + 1) * rows, :] = (
                totals[spot : spot + rows, :] + totals[spot + 4 * rows : spot + 5 * rows, :]
            )
    pl.semaphore_wait(barrier, 4)
    copies = []
    for side in range(4):
        copies.append(
            pltpu.make_async_remote_copy(
                src_ref=outgoing.at[side],
                dst_ref=landing.at[side],
                send_sem=send_sem.at[side],
                recv_sem=recv_sem.at[side],
                device_id=beside[side],
                device_id_type=mesh_ids,
            )
        )
    for copy in copies:
        copy.start()
    add_up(0, rows)
    for copy in copies:
        copy.wait()
    sums = []
    for item in range(4):
        spot = 2 * item * rows
        value = totals[spot : spot + rows, :] + totals[spot + rows : spot + 2 * rows, :]
        for side in range(4):
            value = value + landing[side, item * rows : (item + 1) * rows, :]
        sums.append(value)
    scale = drag_ref[...] * (sums[3] + CORE_LENGTH)
    for item in range(3):
        out_ref[item] = sums[item] / scale


def nodal_call(nx, ny, half, node, owner, drag):
    segs = node.shape[1]
    rows = drag.shape[0]
    vmem = pl.BlockSpec(memory_space=pltpu.VMEM)
    return pl.pallas_call(
        functools.partial(nodal_kernel, nx, ny),
        out_shape=jax.ShapeDtypeStruct((3, rows, NODE_COLS), f32),
        in_specs=[vmem] * 4,
        out_specs=vmem,
        scratch_shapes=[
            pltpu.VMEM((NODE_COLS, 2 * segs), bf16),
            pltpu.VMEM((32 * rows, CHUNK), bf16),
            pltpu.VMEM((32 * rows, NODE_COLS), f32),
            pltpu.VMEM((4, 4 * rows, NODE_COLS), f32),
            pltpu.VMEM((4, 4 * rows, NODE_COLS), f32),
            pltpu.SemaphoreType.DMA((4,)),
            pltpu.SemaphoreType.DMA((4,)),
        ],
        compiler_params=pltpu.CompilerParams(
            collective_id=1, has_side_effects=True, vmem_limit_bytes=48 * 1024 * 1024
        ),
    )(half, node, owner, drag)


def on_device(
    offsets,
    line,
    burgers_kind,
    seg_cell,
    end_node,
    end_owner,
    drag,
    applied,
    pair_list,
    ghost_x_list,
    ghost_y_list,
):
    nx = lax.axis_size("gx")
    ny = lax.axis_size("gy")
    pairs = pair_list[0, 0]
    blocks = offsets.shape[-1] // SEG
    ghosts, base = exchange_call(
        nx,
        ny,
        offsets[0, 0],
        line[0, 0],
        burgers_kind[0],
        seg_cell[0],
        applied,
        ghost_x_list[0, 0],
        ghost_y_list[0, 0],
    )
    count = jnp.sum((pairs[0] < blocks).astype(jnp.int32)).reshape(1)
    half = near_call(count, pairs, ghosts.reshape(-1, SEG), base)
    drag_rows = drag[0, 0].reshape(-1, NODE_COLS)
    velocity = nodal_call(nx, ny, half, end_node[0, 0], end_owner[0, 0], drag_rows)
    return velocity.reshape(1, 1, 3, -1)


def solution(mesh):
    return jax.shard_map(
        on_device,
        mesh=mesh,
        in_specs=(
            P("gx", "gy", None, None),
            P("gx", "gy", None, None),
            P("gx", "gy", None),
            P("gx", "gy", None),
            P("gx", "gy", None, None),
            P("gx", "gy", None, None),
            P("gx", "gy", None),
            P(),
            P("gx", "gy", None, None),
            P("gx", "gy", None, None),
            P("gx", "gy", None, None),
        ),
        out_specs=P("gx", "gy", None, None),
        check_vma=False,
    )
```

time: 1350 us -> 226 us (0.17)
  other arithmetic: 430 us -> 1.39 us
  blocking collectives: 348 us -> 0 us
  Pallas kernels: 0 us -> 221 us
  waiting for transfers between devices: 196 us -> 0 us
  starting transfers between devices: 188 us -> 0 us
  local copies, waits for them, and re-layouts: 153 us -> 3.12 us
  loops' own time: 20.7 us -> 0 us
    all_gather x1 -> x0, blocking collectives: 348 us -> none  [on_device(): lax.all_gather(own_moments[None], ('gx', 'gy'), axis=0, tiled=True)]
    reduce_sum x81 -> x1, other arithmetic: 248 us -> 0.64 us  [on_device(): count = jnp.sum((pairs[0] < blocks).astype(jnp.int32)).reshape(1)]
    pallas_call x0 -> x3, Pallas kernels: none -> 221 us  [the longest x1 86.9 us: nodal_call(): pl.pallas_call(functools.partial(nodal_kernel, nx, ny), out_shape=jax.Sha...]
    ppermute x8 -> x0, waiting for transfers between devices: 196 us -> none  [the longest x4 193 us: with_halo(): lax.ppermute(tail, axis, [(i, (i + 1) % count) for i in range(count)])]
    ppermute x8 -> x0, starting transfers between devices: 188 us -> none  [the longest x4 171 us: with_halo(): lax.ppermute(tail, axis, [(i, (i + 1) % count) for i in range(count)])]
    scatter-add x70 -> x0, other arithmetic: 156 us -> none  [the longest x2 106 us: nodal_terms(): jnp.zeros((4, 5 * nodes), jnp.float32).at[:, slot_start].add(half)]
    gather x132 -> x0, local copies, waits for them, and re-layouts: 72.5 us -> none  [the longest x64 35.5 us: group_stress(): target_data = owned[:, jnp.clip(targets, 0, blocks - 1)]]
    another operation x2 -> x0, loops' own time: 20.7 us -> none  [the longest x1 10.4 us: on_device(): lax.fori_loop(0, turns, body_step, jnp.zeros((6, blocks, data.shape[2]),...]
  transfers between devices with their start and end apart: 8 -> 0, of which waited for: 4 -> 0; matrix products, arithmetic and copies ran while one was open for 6% -> 0% of each run, Pallas kernels for 0% -> 0%
where the time goes in v1:
time: 226 us; the launch traced here: 225 us
  Pallas kernels  221 us (98%)
  local copies, waits for them, and re-layouts  3.12 us (1%)
    pallas_call x1, Pallas kernels, nodal_call(): pl.pallas_call(functools.partial(nodal_kernel, nx, ny), out_shape=jax.Sha...  86.9 us
    pallas_call x1, Pallas kernels, near_call(): pl.pallas_call(functools.partial(near_kernel, blocks, number), out_shape=...  84.6 us
    pallas_call x1, Pallas kernels, exchange_call(): pl.pallas_call(functools.partial(exchange_kernel, nx, ny), out_shape=(jax...  49.1 us

profile of v1, /device:TPU:32, one launch (start us, length us, event | category | flops | bytes accessed | tf_op | source)
XLA Modules:
  0.0 225.2 jit_solution(3115022633250417993)
XLA Ops:
  0.0 0.0 copy-start.2
  0.0 0.0 copy-start.3
  0.0 1.1 copy_bitcast_fusion
  1.1 0.0 copy-start.6
  1.1 0.0 copy-start.5
  1.1 0.0 copy-start.7
  1.1 0.0 copy-done.2
  1.1 0.0 copy-done.3
  1.1 0.6 copy-done.6
  1.8 0.0 copy-done.5
  1.8 0.0 copy-done.7
  1.8 0.0 copy-start.4
  1.8 49.1 %shard_map.109 = (f32[192,8,128]{2,1,0:T(8,128)S(1)}, f32[8,8192]{1,0:T(8,128)S(1)}) custom-call(f32[3,8192]{1,0:T(4,128)S(1)} %get-tuple-element.10.off_ref, f32[3,8192]{1,0:T(4,128)S(1)} %get-tuple-element.9.line_ref, s32[1,8192]{1,0:T(1,128)S(1)} %bitcast.16, s32[1,8192]{1,0:T(1,128)S(1)} %bitcast.17, f32[6]{0:T(128)S(1)} %copy-done.7, ...), custom_call_target="tpu_custom_call" | custom-call | tf_op jit(solution)/shard_map/pallas_call | solution.py:639
  50.9 0.0 copy-done.4
  50.9 0.6 fusion
  51.6 0.0 copy-start.8
  51.6 84.6 %shard_map.110.half_ref = f32[512,128]{1,0:T(8,128)S(1)} custom-call(s32[1]{0:T(128)} %bitcast.count_ref, s32[2,1024]{1,0:T(2,128)S(1)} %bitcast.18, f32[1536,128]{1,0:T(8,128)S(1)} %bitcast.13, f32[8,8192]{1,0:T(8,128)S(1)} %get-tuple-element.8.base_ref), custom_call_target="tpu_custom_call" | custom-call | tf_op jit(solution)/shard_map/pallas_call | solution.py:256
  136.2 0.5 broadcast.5
  136.7 0.0 copy-done.8
  136.7 0.0 copy-start
  136.7 0.0 copy-start.1
  136.7 0.8 reduce.4
  137.5 0.1 copy-done
  137.5 0.0 copy-done.1
  137.6 86.9 %shard_map.111 = f32[3,32,256]{2,1,0:T(8,128)S(1)} custom-call(f32[512,128]{1,0:T(8,128)S(1)} %shard_map.110.half_ref, s32[2,8192]{1,0:T(2,128)S(1)} %bitcast.14, s32[2,8192]{1,0:T(2,128)S(1)} %bitcast.15, f32[32,256]{1,0:T(8,128)S(1)} %reshape_squeeze.3.drag_ref), custom_call_target="tpu_custom_call" | custom-call | tf_op jit(solution)/shard_map/pallas_call | solution.py:799
  224.5 0.7 reshape.17
  (1 shorter events, 0.0 us)
Async XLA Ops:
  0.0 1.1 copy-start.2
  0.0 1.1 copy-start.3
  1.1 0.7 copy-start.6
  1.1 0.7 copy-start.5
  1.1 0.7 copy-start.7
  1.8 49.1 %copy-start.4 = (s32[1,1,2,1024]{3,2,1,0:T(2,128)S(1)}, s32[1,1,2,1024]{3,2,1,0:T(2,128)}, u32[]{:S(2)}) copy-start(s32[1,1,2,1024]{3,2,1,0:T(2,128)} %param.19) | copy-start | bytes 24580
  51.6 85.1 %copy-start.8 = (f32[1,1,8192]{2,1,0:T(1,128)S(1)}, f32[1,1,8192]{2,1,0:T(1,128)}, u32[]{:S(2)}) copy-start(f32[1,1,8192]{2,1,0:T(1,128)} %param.17) | copy-start | bytes 98308
  136.7 0.8 copy-start
  136.7 0.9 copy-start.1

commit v2 on v1

--- a/solution.py
+++ b/solution.py
@@ -33,7 +33,7 @@
     ((1.0, 0, (0, 1, 2)), (1.0, 1, (1, 1, 2)), (-1.0, 2, (0, 0, 1)), (-1.0, 2, (1, 1, 1))),
 )
 CENTER = (CCX / 2.0, CCY / 2.0, NCZ / 2.0)
-UNROLL = 4
+UNROLL = 32
 TRANSPOSED = (((1,), (1,)), ((), ()))
 f32 = jnp.float32
 bf16 = jnp.bfloat16
@@ -125,25 +125,32 @@
 
 
 def near_kernel(
-    blocks, ghosts, count_ref, pairs_ref, gh_ref, base_ref, out_ref, xb, qt, acc, scr3, scr5
+    blocks, ghosts, count_ref, pairs_ref, gh_ref, base_ref, out_ref, xb, qt, acc
 ):
     zero = jnp.zeros((SEG, SEG), f32)
-    for part in range(8):
-        scr3[pl.ds(part * SEG, SEG), :] = zero
-        scr5[pl.ds(part * SEG, SEG), :] = zero
+    blank = jnp.zeros((8, SEG), f32)
 
     def source_step(group, carry):
         first = pl.multiple_of(group * 64, 64)
         rows = [gh_ref[pl.ds(first + row, 8, stride=8), :] for row in range(7)]
+        spots3 = [blank] * 40
+        spots5 = [blank] * 40
         for spot, term3, term5 in source_columns(rows[0:3], rows[3:6], rows[6]):
-            for shift, piece in zip((0, 40, 80), parts_of(term5)):
-                scr5[pl.ds(spot + shift, 8, stride=SEG), :] = piece
+            spots5[spot] = term5
             if term3 is not None:
-                for shift, piece in zip((0, 40, 80), parts_of(term3)):
-                    scr3[pl.ds(spot + shift, 8, stride=SEG), :] = piece
-        for part in range(8):
-            qt[group * 8 + part, :, 0:SEG] = scr3[pl.ds(part * SEG, SEG), :].astype(bf16)
-            qt[group * 8 + part, :, SEG : 2 * SEG] = scr5[pl.ds(part * SEG, SEG), :].astype(bf16)
+                spots3[spot] = term3
+        for half, spots, size in ((0, spots3, 32), (1, spots5, 40)):
+            swapped = jnp.transpose(jnp.stack(spots[:size], axis=0), (1, 0, 2))
+            for part in range(8):
+                pieces = []
+                for piece in parts_of(swapped[part]):
+                    pieces.append(piece)
+                    if size < 40:
+                        pieces.append(blank)
+                pieces.append(blank)
+                qt[group * 8 + part, :, half * SEG : half * SEG + SEG] = jnp.concatenate(
+                    pieces, axis=0
+                ).astype(bf16)
         return carry
 
     lax.fori_loop(0, ghosts // 8, source_step, 0)
@@ -156,7 +163,7 @@
         acc[block] = zero
         return carry
 
-    lax.fori_loop(0, blocks, target_step, 0)
+    lax.fori_loop(0, blocks, target_step, 0, unroll=4)
 
     def pair_step(turn, carry):
         for part in range(UNROLL):
@@ -247,7 +254,7 @@
         )
         return carry
 
-    lax.fori_loop(0, blocks, force_step, 0)
+    lax.fori_loop(0, blocks, force_step, 0, unroll=4)
 
 
 def near_call(count, pairs, ghosts, base):
@@ -267,8 +274,6 @@
             pltpu.VMEM((3 * blocks, SEG, SEG), f32),
             pltpu.VMEM((number, SEG, 2 * SEG), bf16),
             pltpu.VMEM((blocks, SEG, SEG), f32),
-            pltpu.VMEM((8 * SEG, SEG), f32),
-            pltpu.VMEM((8 * SEG, SEG), f32),
         ],
         compiler_params=pltpu.CompilerParams(vmem_limit_bytes=48 * 1024 * 1024),
     )(count, pairs, ghosts, base)
@@ -670,7 +675,7 @@
 
 
 NODE_COLS = 256
-CHUNK = 2048
+CHUNK = 1024
 
 
 def nodal_kernel(
@@ -714,46 +719,53 @@
             column_hot[:, where] = (column_iota == column).astype(f32).astype(bf16)
         return carry
 
-    lax.fori_loop(0, segs // SEG, column_step, 0)
+    lax.fori_loop(0, segs // SEG, column_step, 0, unroll=2)
+
+    tiles = CHUNK // SEG
+    chunks = 2 * segs // CHUNK
 
     def add_up(first_row, count):
         row_iota = lax.broadcasted_iota(jnp.int32, (count, SEG), 0) + first_row
 
-        def chunk_step(chunk, carry):
-            for end in range(2):
-
-                def tile_step(tile, inner):
-                    block = chunk * (CHUNK // SEG) + tile
-                    lanes = pl.ds(pl.multiple_of(block * SEG, SEG), SEG)
-                    slot = (
-                        owner_ref[end : end + 1, lanes] * rows
-                        + node_ref[end : end + 1, lanes] // NODE_COLS
-                    )
-                    mask = row_iota == slot
-                    values = half_ref[pl.ds(pl.multiple_of(block * 8, 8), 8), :]
-                    heads = values.astype(bf16).astype(f32)
-                    tails = values - heads
-                    where = pl.ds(pl.multiple_of(tile * SEG, SEG), SEG)
-                    for item in range(4):
-                        for part, piece in enumerate((heads, tails)):
-                            spot = (2 * item + part) * count
-                            row_hot[spot : spot + count, where] = jnp.where(
-                                mask, piece[item : item + 1], 0.0
-                            ).astype(bf16)
-                    return inner
-
-                lax.fori_loop(0, CHUNK // SEG, tile_step, 0)
-                where = pl.ds(pl.multiple_of(end * segs + chunk * CHUNK, CHUNK), CHUNK)
-                totals[0 : 8 * count, :] = totals[0 : 8 * count, :] + lax.dot_general(
-                    row_hot[0 : 8 * count, :],
-                    column_hot[:, where],
-                    TRANSPOSED,
-                    preferred_element_type=f32,
-                )
+        def build(buffer, chunk):
+            end = chunk // (segs // CHUNK)
+            for tile in range(tiles):
+                block = chunk % (segs // CHUNK) * tiles + tile
+                lanes = pl.ds(pl.multiple_of(block * SEG, SEG), SEG)
+                both = owner_ref[:, lanes] * rows + node_ref[:, lanes] // NODE_COLS
+                slot = jnp.where(end == 0, both[0:1], both[1:2])
+                mask = (row_iota == slot).astype(f32).astype(bf16)
+                values = half_ref[pl.ds(pl.multiple_of(block * 8, 8), 8), :]
+                heads = values.astype(bf16).astype(f32)
+                tails = values - heads
+                for item in range(4):
+                    for part, piece in enumerate((heads, tails)):
+                        spot = (2 * item + part) * count
+                        row = jnp.broadcast_to(piece[item : item + 1], (16, SEG)).astype(bf16)
+                        row = jnp.concatenate([row] * (count // 16), axis=0)
+                        row_hot[buffer, spot : spot + count, tile * SEG : (tile + 1) * SEG] = (
+                            mask * row
+                        )
+
+        def add_chunk(buffer, chunk):
+            where = pl.ds(pl.multiple_of(chunk * CHUNK, CHUNK), CHUNK)
+            totals[0 : 8 * count, :] = totals[0 : 8 * count, :] + lax.dot_general(
+                row_hot[buffer, 0 : 8 * count, :],
+                column_hot[:, where],
+                TRANSPOSED,
+                preferred_element_type=f32,
+            )
+
+        def chunk_step(turn, carry):
+            build(1, 2 * turn + 1)
+            add_chunk(0, 2 * turn)
+            build(0, jnp.minimum(2 * turn + 2, chunks - 1))
+            add_chunk(1, 2 * turn + 1)
             return carry
 
         totals[0 : 8 * count, :] = jnp.zeros((8 * count, NODE_COLS), f32)
-        lax.fori_loop(0, segs // CHUNK, chunk_step, 0)
+        build(0, jnp.int32(0))
+        lax.fori_loop(0, chunks // 2, chunk_step, 0)
 
     add_up(rows, 4 * rows)
     for side in range(4):
@@ -803,7 +815,7 @@
         out_specs=vmem,
         scratch_shapes=[
             pltpu.VMEM((NODE_COLS, 2 * segs), bf16),
-            pltpu.VMEM((32 * rows, CHUNK), bf16),
+            pltpu.VMEM((2, 32 * rows, CHUNK), bf16),
             pltpu.VMEM((32 * rows, NODE_COLS), f32),
             pltpu.VMEM((4, 4 * rows, NODE_COLS), f32),
             pltpu.VMEM((4, 4 * rows, NODE_COLS), f32),

time: 226 us -> 146 us (0.65)
  the two profiles are of different devices: /device:TPU:32 before, /device:TPU:54 now
where the time goes in v2:
time: 146 us
  Pallas kernels  141 us (97%)
  local copies, waits for them, and re-layouts  3.12 us (2%)
    pallas_call x1, Pallas kernels, near_call(): pl.pallas_call(functools.partial(near_kernel, blocks, number), out_shape=...  69.2 us
    pallas_call x1, Pallas kernels, exchange_call(): pl.pallas_call(functools.partial(exchange_kernel, nx, ny), out_shape=(jax...  52.4 us
    pallas_call x1, Pallas kernels, nodal_call(): pl.pallas_call(functools.partial(nodal_kernel, nx, ny), out_shape=jax.Sha...  19.4 us

profile of v2, /device:TPU:54, one launch (start us, length us, event | category | flops | bytes accessed | tf_op | source)
XLA Modules:
  0.0 145.6 jit_solution(13489972670870514114)
XLA Ops:
  0.0 0.0 copy-start.2
  0.0 0.0 copy-start.3
  0.0 1.1 copy_bitcast_fusion
  1.1 0.0 copy-start.6
  1.1 0.0 copy-start.5
  1.1 0.0 copy-start.7
  1.1 0.0 copy-done.2
  1.1 0.0 copy-done.3
  1.1 0.6 copy-done.6
  1.8 0.0 copy-done.5
  1.8 0.0 copy-done.7
  1.8 0.0 copy-start.4
  1.8 52.4 %shard_map.109 = (f32[192,8,128]{2,1,0:T(8,128)S(1)}, f32[8,8192]{1,0:T(8,128)S(1)}) custom-call(f32[3,8192]{1,0:T(4,128)S(1)} %get-tuple-element.10.off_ref, f32[3,8192]{1,0:T(4,128)S(1)} %get-tuple-element.9.line_ref, s32[1,8192]{1,0:T(1,128)S(1)} %bitcast.16, s32[1,8192]{1,0:T(1,128)S(1)} %bitcast.17, f32[6]{0:T(128)S(1)} %copy-done.7, ...), custom_call_target="tpu_custom_call" | custom-call | tf_op jit(solution)/shard_map/pallas_call | solution.py:644
  54.2 0.0 copy-done.4
  54.2 0.6 fusion
  54.9 0.0 copy-start.8
  54.9 69.2 %shard_map.110.half_ref = f32[512,128]{1,0:T(8,128)S(1)} custom-call(s32[1]{0:T(128)} %bitcast.count_ref, s32[2,1024]{1,0:T(2,128)S(1)} %bitcast.18, f32[1536,128]{1,0:T(8,128)S(1)} %bitcast.13, f32[8,8192]{1,0:T(8,128)S(1)} %get-tuple-element.8.base_ref), custom_call_target="tpu_custom_call" | custom-call | tf_op jit(solution)/shard_map/pallas_call | solution.py:263
  124.1 0.5 broadcast.5
  124.6 0.0 copy-done.8
  124.6 0.0 copy-start
  124.6 0.0 copy-start.1
  124.6 0.8 reduce.4
  125.4 0.1 copy-done
  125.4 0.0 copy-done.1
  125.5 19.4 %shard_map.111 = f32[3,32,256]{2,1,0:T(8,128)S(1)} custom-call(f32[512,128]{1,0:T(8,128)S(1)} %shard_map.110.half_ref, s32[2,8192]{1,0:T(2,128)S(1)} %bitcast.14, s32[2,8192]{1,0:T(2,128)S(1)} %bitcast.15, f32[32,256]{1,0:T(8,128)S(1)} %reshape_squeeze.3.drag_ref), custom_call_target="tpu_custom_call" | custom-call | tf_op jit(solution)/shard_map/pallas_call | solution.py:811
  144.9 0.7 reshape.17
  (1 shorter events, 0.0 us)
Async XLA Ops:
  0.0 1.1 copy-start.2
  0.0 1.1 copy-start.3
  1.1 0.7 copy-start.6
  1.1 0.7 copy-start.5
  1.1 0.7 copy-start.7
  1.8 52.4 %copy-start.4 = (s32[1,1,2,1024]{3,2,1,0:T(2,128)S(1)}, s32[1,1,2,1024]{3,2,1,0:T(2,128)}, u32[]{:S(2)}) copy-start(s32[1,1,2,1024]{3,2,1,0:T(2,128)} %param.19) | copy-start | bytes 24580
  54.9 69.7 %copy-start.8 = (f32[1,1,8192]{2,1,0:T(1,128)S(1)}, f32[1,1,8192]{2,1,0:T(1,128)}, u32[]{:S(2)}) copy-start(f32[1,1,8192]{2,1,0:T(1,128)} %param.17) | copy-start | bytes 98308
  124.6 0.8 copy-start
  124.6 0.9 copy-start.1

commit v3 on v2

--- a/solution.py
+++ b/solution.py
@@ -34,6 +34,7 @@
 )
 CENTER = (CCX / 2.0, CCY / 2.0, NCZ / 2.0)
 UNROLL = 32
+PAIR_STEP = 256
 TRANSPOSED = (((1,), (1,)), ((), ()))
 f32 = jnp.float32
 bf16 = jnp.bfloat16
@@ -125,7 +126,7 @@
 
 
 def near_kernel(
-    blocks, ghosts, count_ref, pairs_ref, gh_ref, base_ref, out_ref, xb, qt, acc
+    blocks, ghosts, pairs_ref, gh_ref, base_ref, out_ref, xb, qt, acc
 ):
     zero = jnp.zeros((SEG, SEG), f32)
     blank = jnp.zeros((8, SEG), f32)
@@ -153,17 +154,20 @@
                 ).astype(bf16)
         return carry
 
-    lax.fori_loop(0, ghosts // 8, source_step, 0)
-
-    def target_step(block, carry):
+    def target_step(block):
         tile = gh_ref[pl.ds(pl.multiple_of(block * 8, 8), 8), :]
         columns = jnp.transpose(tile)
         for axis in range(3):
             xb[3 * block + axis] = jnp.broadcast_to(columns[:, axis : axis + 1], (SEG, SEG))
         acc[block] = zero
-        return carry
-
-    lax.fori_loop(0, blocks, target_step, 0, unroll=4)
+
+    def both_step(group, carry):
+        for part in range(8):
+            target_step(group * 8 + part)
+        return source_step(group, carry)
+
+    lax.fori_loop(0, blocks // 8, both_step, 0)
+    lax.fori_loop(blocks // 8, ghosts // 8, source_step, 0)
 
     def pair_step(turn, carry):
         for part in range(UNROLL):
@@ -201,7 +205,10 @@
             acc[target] = acc[target] + piece
         return carry
 
-    lax.fori_loop(0, count_ref[0] // UNROLL, pair_step, 0)
+    turns = jnp.int32(0)
+    for first in range(0, pairs_ref.shape[1], PAIR_STEP):
+        turns = turns + jnp.where(pairs_ref[0, first] < blocks, PAIR_STEP // UNROLL, 0)
+    lax.fori_loop(0, turns, pair_step, 0)
 
     def force_step(block, carry):
         first = pl.multiple_of(block * 8, 8)
@@ -254,17 +261,16 @@
         )
         return carry
 
-    lax.fori_loop(0, blocks, force_step, 0, unroll=4)
-
-
-def near_call(count, pairs, ghosts, base):
+    lax.fori_loop(0, blocks, force_step, 0, unroll=8)
+
+
+def near_call(pairs, ghosts, base):
     blocks = base.shape[1] // SEG
     number = ghosts.shape[0] // 8
     return pl.pallas_call(
         functools.partial(near_kernel, blocks, number),
         out_shape=jax.ShapeDtypeStruct((blocks * 8, SEG), f32),
         in_specs=[
-            pl.BlockSpec(memory_space=pltpu.SMEM),
             pl.BlockSpec(memory_space=pltpu.SMEM),
             pl.BlockSpec(memory_space=pltpu.VMEM),
             pl.BlockSpec(memory_space=pltpu.VMEM),
@@ -276,7 +282,7 @@
             pltpu.VMEM((blocks, SEG, SEG), f32),
         ],
         compiler_params=pltpu.CompilerParams(vmem_limit_bytes=48 * 1024 * 1024),
-    )(count, pairs, ghosts, base)
+    )(pairs, ghosts, base)
 
 
 def wrapped(diff, extent):
@@ -354,20 +360,34 @@
     mesh_ids = pl.DeviceIdType.MESH
     barrier = pltpu.get_barrier_semaphore()
 
-    def greet_x(step, carry):
-        pl.semaphore_signal(
-            barrier, inc=1, device_id=(lax.rem(me_x + step, nx), me_y), device_id_type=mesh_ids
-        )
-        return carry
-
-    def greet_y(step, carry):
-        pl.semaphore_signal(
-            barrier, inc=1, device_id=(me_x, lax.rem(me_y + step, ny)), device_id_type=mesh_ids
-        )
-        return carry
-
-    lax.fori_loop(1, nx, greet_x, 0)
-    lax.fori_loop(1, ny, greet_y, 0)
+    half_x = nx // 2
+    high = me_x // half_x
+    spot = me_x % half_x
+    column = high * ny + me_y
+    depth_count = 2 * ny
+
+    def column_device(step):
+        other = lax.rem(column + step, depth_count)
+        return (other // ny * half_x + spot, other % ny)
+
+    def plane_device(step):
+        return (high * half_x + lax.rem(spot + step, half_x), me_y)
+
+    def greet(device):
+        pl.semaphore_signal(barrier, inc=1, device_id=device, device_id_type=mesh_ids)
+
+    def greet_column(step, carry):
+        greet(column_device(step))
+        return carry
+
+    def greet_plane(step, carry):
+        greet(plane_device(step))
+        return carry
+
+    lax.fori_loop(1, depth_count, greet_column, 0)
+    lax.fori_loop(1, half_x, greet_plane, 0)
+    greet((lax.rem(me_x + nx - 1, nx), me_y))
+    greet((lax.rem(me_x + 1, nx), me_y))
 
     cell_iota = lax.broadcasted_iota(jnp.int32, (cells, SEG), 0)
     origin = [0.5 - CENTER[axis] for axis in range(3)]
@@ -396,7 +416,7 @@
         hot[:, lanes] = (cell_iota == cell).astype(f32).astype(bf16)
         return carry
 
-    lax.fori_loop(0, blocks, block_step, 0)
+    lax.fori_loop(0, blocks, block_step, 0, unroll=4)
 
     def pick_x(item, carry):
         for side in range(2):
@@ -404,8 +424,13 @@
             pack_x[side, item] = gh_ref[source]
         return carry
 
-    lax.fori_loop(0, packet, pick_x, 0)
-    pl.semaphore_wait(barrier, nx - 1 + ny - 1)
+    lax.fori_loop(0, packet, pick_x, 0, unroll=8)
+    moments = lax.dot_general(products[...], hot[...], TRANSPOSED, preferred_element_type=f32)
+    moments = moments[0:16] + moments[16:32] + moments[32:48]
+    mine[...] = jnp.concatenate([moments, jnp.zeros((16, SEG - cells), f32)], axis=1)
+    row_land[column] = mine[...]
+
+    pl.semaphore_wait(barrier, depth_count - 1 + half_x - 1 + 2)
 
     copies_x = []
     for side in range(2):
@@ -423,18 +448,13 @@
     for copy in copies_x:
         copy.start()
 
-    moments = lax.dot_general(products[...], hot[...], TRANSPOSED, preferred_element_type=f32)
-    moments = moments[0:16] + moments[16:32] + moments[32:48]
-    mine[...] = jnp.concatenate([moments, jnp.zeros((16, SEG - cells), f32)], axis=1)
-    row_land[me_y] = mine[...]
-
     def row_copy(step):
         return pltpu.make_async_remote_copy(
             src_ref=mine,
-            dst_ref=row_land.at[me_y],
+            dst_ref=row_land.at[column],
             send_sem=row_send.at[step],
             recv_sem=row_recv.at[step],
-            device_id=(me_x, lax.rem(me_y + step, ny)),
+            device_id=column_device(step),
             device_id_type=mesh_ids,
         )
 
@@ -446,7 +466,7 @@
         row_copy(step).wait()
         return carry
 
-    lax.fori_loop(1, ny, row_start, 0)
+    lax.fori_loop(1, depth_count, row_start, 0)
 
     row_iota = lax.broadcasted_iota(jnp.int32, (8, SEG), 0)
     for copy in copies_x:
@@ -458,7 +478,7 @@
             gh_ref[blocks + slot * packet + item] = land_x[slot, item] + moved
             return carry
 
-        lax.fori_loop(0, packet, take_x, 0)
+        lax.fori_loop(0, packet, take_x, 0, unroll=8)
 
     def pick_y(item, carry):
         for side in range(2):
@@ -466,7 +486,7 @@
             pack_y[side, item] = gh_ref[source]
         return carry
 
-    lax.fori_loop(0, packet, pick_y, 0)
+    lax.fori_loop(0, packet, pick_y, 0, unroll=8)
     copies_y = []
     for side in range(2):
         target = lax.rem(me_y + (ny - 1 if side == 0 else 1), ny)
@@ -483,37 +503,42 @@
     for copy in copies_y:
         copy.start()
 
-    lax.fori_loop(1, ny, row_wait, 0)
+    lax.fori_loop(1, depth_count, row_wait, 0)
     lane_iota = lax.broadcasted_iota(jnp.int32, (16, SEG), 1)
-    lasts = []
-    for tile in range(4):
-        first = row_land[2 * tile]
-        second = row_land[2 * tile + 1]
-        merged = jnp.where(lane_iota < cells, first, pltpu.roll(second, cells, 1))
-        row_block[8 * tile : 8 * tile + 8, :] = merged[0:8]
-        lasts.append(merged[8:9])
-    row_block[32:40, :] = jnp.concatenate(lasts + [jnp.zeros((4, SEG), f32)], axis=0)
-    all_land[me_x] = row_block[...]
+    for part in range(2):
+        lasts = []
+        for tile in range(4):
+            first = row_land[part * ny + 2 * tile]
+            second = row_land[part * ny + 2 * tile + 1]
+            merged = jnp.where(lane_iota < cells, first, pltpu.roll(second, cells, 1))
+            row_block[40 * part + 8 * tile : 40 * part + 8 * tile + 8, :] = merged[0:8]
+            lasts.append(merged[8:9])
+        row_block[40 * part + 32 : 40 * part + 40, :] = jnp.concatenate(
+            lasts + [jnp.zeros((4, SEG), f32)], axis=0
+        )
+    all_land[spot] = row_block[...]
 
     def all_copy(step):
         return pltpu.make_async_remote_copy(
             src_ref=row_block,
-            dst_ref=all_land.at[me_x],
+            dst_ref=all_land.at[spot],
             send_sem=all_send.at[step],
             recv_sem=all_recv.at[step],
-            device_id=(lax.rem(me_x + step, nx), me_y),
+            device_id=plane_device(step),
             device_id_type=mesh_ids,
         )
 
     def all_start(step, carry):
         all_copy(step).start()
-        return carry
-
-    def all_wait(step, carry):
-        all_copy(step).wait()
-        return carry
-
-    lax.fori_loop(1, nx, all_start, 0)
+        all_copy(half_x - step).start()
+        return carry
+
+    def all_sent(step, carry):
+        all_copy(step).wait_send()
+        return carry
+
+    lax.fori_loop(1, half_x // 2, all_start, 0)
+    all_copy(half_x // 2).start()
 
     for copy in copies_y:
         copy.wait()
@@ -524,10 +549,9 @@
             gh_ref[blocks + (2 + slot) * packet + item] = land_y[slot, item] + moved
             return carry
 
-        lax.fori_loop(0, packet, take_y, 0)
+        lax.fori_loop(0, packet, take_y, 0, unroll=8)
 
     far_acc[...] = jnp.zeros_like(far_acc)
-    lax.fori_loop(1, nx, all_wait, 0)
 
     lane = lax.broadcasted_iota(jnp.int32, (8, SEG), 1)
     source_z = (lane % NCZ).astype(f32)
@@ -536,9 +560,7 @@
     ]
     extent_y = float(CCY * ny)
 
-    def far_step(turn, carry):
-        apart = turn // 4
-        tile = turn % 4
+    def far_step(apart, tile):
         step = apart.astype(f32)
         middle = apart == nx // 2
         upper = me_x >= nx // 2
@@ -546,13 +568,21 @@
         weight_minus = jnp.where((apart == 0) | (middle & upper), 0.0, 1.0)
         place_plus = lax.rem(me_x - apart + nx, nx)
         place_minus = lax.rem(me_x + apart, nx)
-        rows = pl.ds(pl.multiple_of(tile * 8, 8), 8)
-        head_plus = all_land[place_plus, rows, :] * weight_plus
-        head_minus = all_land[place_minus, rows, :] * weight_minus
+        spot_plus = place_plus % half_x
+        spot_minus = place_minus % half_x
+        row_plus = place_plus // half_x * 40
+        row_minus = place_minus // half_x * 40
+        head_plus = (
+            all_land[spot_plus, pl.ds(pl.multiple_of(row_plus + tile * 8, 8), 8), :] * weight_plus
+        )
+        head_minus = (
+            all_land[spot_minus, pl.ds(pl.multiple_of(row_minus + tile * 8, 8), 8), :]
+            * weight_minus
+        )
         plus = [head_plus[item : item + 1] for item in range(8)]
         minus = [head_minus[item : item + 1] for item in range(8)]
-        plus.append(all_land[place_plus, pl.ds(32 + tile, 1), :] * weight_plus)
-        minus.append(all_land[place_minus, pl.ds(32 + tile, 1), :] * weight_minus)
+        plus.append(all_land[spot_plus, pl.ds(row_plus + 32 + tile, 1), :] * weight_plus)
+        minus.append(all_land[spot_minus, pl.ds(row_minus + 32 + tile, 1), :] * weight_minus)
         turned, curls = far_rows(plus, minus, step)
         source_y = (lane // NCZ + tile * 8).astype(f32)
         close = apart <= 1
@@ -591,7 +621,7 @@
                     wave_odd * rz,
                     wave_y * rz,
                 )
-                spot = 8 * (2 * quarter + half)
+                first = 8 * (2 * quarter + half)
                 for comp in range(6):
                     swirl = None
                     for factor, item in zip((None, ry, rz), turned[comp]):
@@ -601,10 +631,31 @@
                     value = gain * swirl + inv_three * bends[comp] - curved[comp]
                     if comp < 3:
                         value = value - trace
-                    far_acc[comp, spot : spot + 8, :] = far_acc[comp, spot : spot + 8, :] + value
-        return carry
-
-    lax.fori_loop(0, 4 * (nx // 2 + 1), far_step, 0)
+                    far_acc[comp, first : first + 8, :] = far_acc[comp, first : first + 8, :] + value
+
+    def far_own(turn, carry):
+        far_step(turn // 4 * half_x, turn % 4)
+        return carry
+
+    def far_columns(near_by, carry):
+        all_copy(near_by).wait_recv()
+        all_copy(half_x - near_by).wait_recv()
+
+        def far_two(turn, inner):
+            far_step(jnp.where(turn < 4, near_by, half_x - near_by), turn % 4)
+            return inner
+
+        return lax.fori_loop(0, 8, far_two, carry)
+
+    def far_last(turn, carry):
+        far_step(jnp.int32(half_x // 2), turn)
+        return carry
+
+    lax.fori_loop(0, 8, far_own, 0)
+    lax.fori_loop(1, half_x // 2, far_columns, 0)
+    all_copy(half_x // 2).wait_recv()
+    lax.fori_loop(0, 4, far_last, 0)
+    lax.fori_loop(1, half_x, all_sent, 0)
 
     pick = (
         lax.broadcasted_iota(jnp.int32, (8, 6 * SEG), 1) // SEG
@@ -657,16 +708,16 @@
             pltpu.VMEM((2, packet, 8, SEG), f32),
             pltpu.VMEM((2, packet, 8, SEG), f32),
             pltpu.VMEM((16, SEG), f32),
-            pltpu.VMEM((ny, 16, SEG), f32),
-            pltpu.VMEM((40, SEG), f32),
-            pltpu.VMEM((nx, 40, SEG), f32),
+            pltpu.VMEM((2 * ny, 16, SEG), f32),
+            pltpu.VMEM((80, SEG), f32),
+            pltpu.VMEM((nx // 2, 80, SEG), f32),
             pltpu.VMEM((6, cells, SEG), f32),
             pltpu.SemaphoreType.DMA((4,)),
             pltpu.SemaphoreType.DMA((4,)),
-            pltpu.SemaphoreType.DMA((ny,)),
-            pltpu.SemaphoreType.DMA((ny,)),
-            pltpu.SemaphoreType.DMA((nx,)),
-            pltpu.SemaphoreType.DMA((nx,)),
+            pltpu.SemaphoreType.DMA((2 * ny,)),
+            pltpu.SemaphoreType.DMA((2 * ny,)),
+            pltpu.SemaphoreType.DMA((nx // 2,)),
+            pltpu.SemaphoreType.DMA((nx // 2,)),
         ],
         compiler_params=pltpu.CompilerParams(
             collective_id=0, has_side_effects=True, vmem_limit_bytes=32 * 1024 * 1024
@@ -695,7 +746,7 @@
     recv_sem,
 ):
     segs = node_ref.shape[1]
-    rows = drag_ref.shape[0]
+    rows = drag_ref.shape[1] // NODE_COLS
     me_x = lax.axis_index("gx")
     me_y = lax.axis_index("gy")
     mesh_ids = pl.DeviceIdType.MESH
@@ -799,18 +850,24 @@
         for side in range(4):
             value = value + landing[side, item * rows : (item + 1) * rows, :]
         sums.append(value)
-    scale = drag_ref[...] * (sums[3] + CORE_LENGTH)
-    for item in range(3):
-        out_ref[item] = sums[item] / scale
+    drag = jnp.concatenate(
+        [drag_ref[:, row * NODE_COLS : (row + 1) * NODE_COLS] for row in range(rows)], axis=0
+    )
+    scale = 1.0 / (drag * (sums[3] + CORE_LENGTH))
+    speed = [sums[item] * scale for item in range(3)]
+    for row in range(rows):
+        out_ref[:, row * NODE_COLS : (row + 1) * NODE_COLS] = jnp.concatenate(
+            [piece[row : row + 1] for piece in speed], axis=0
+        )
 
 
 def nodal_call(nx, ny, half, node, owner, drag):
     segs = node.shape[1]
-    rows = drag.shape[0]
+    rows = drag.shape[1] // NODE_COLS
     vmem = pl.BlockSpec(memory_space=pltpu.VMEM)
     return pl.pallas_call(
         functools.partial(nodal_kernel, nx, ny),
-        out_shape=jax.ShapeDtypeStruct((3, rows, NODE_COLS), f32),
+        out_shape=jax.ShapeDtypeStruct((3, drag.shape[1]), f32),
         in_specs=[vmem] * 4,
         out_specs=vmem,
         scratch_shapes=[
@@ -844,7 +901,6 @@
     nx = lax.axis_size("gx")
     ny = lax.axis_size("gy")
     pairs = pair_list[0, 0]
-    blocks = offsets.shape[-1] // SEG
     ghosts, base = exchange_call(
         nx,
         ny,
@@ -856,11 +912,9 @@
         ghost_x_list[0, 0],
         ghost_y_list[0, 0],
     )
-    count = jnp.sum((pairs[0] < blocks).astype(jnp.int32)).reshape(1)
-    half = near_call(count, pairs, ghosts.reshape(-1, SEG), base)
-    drag_rows = drag[0, 0].reshape(-1, NODE_COLS)
-    velocity = nodal_call(nx, ny, half, end_node[0, 0], end_owner[0, 0], drag_rows)
-    return velocity.reshape(1, 1, 3, -1)
+    half = near_call(pairs, ghosts.reshape(-1, SEG), base)
+    velocity = nodal_call(nx, ny, half, end_node[0, 0], end_owner[0, 0], drag[0])
+    return velocity[None, None]
 
 
 def solution(mesh):

time: 146 us -> 131 us (0.90)
  the two profiles are of different devices: /device:TPU:54 before, /device:TPU:32 now
where the time goes in v3:
time: 131 us; the launch traced here: 130 us
  Pallas kernels  128 us (98%)
  local copies, waits for them, and re-layouts  2.51 us (2%)
    pallas_call x1, Pallas kernels, nodal_call(): pl.pallas_call(functools.partial(nodal_kernel, nx, ny), out_shape=jax.Sha...  49.7 us
    pallas_call x1, Pallas kernels, near_call(): pl.pallas_call(functools.partial(near_kernel, blocks, number), out_shape=...  39.1 us
    pallas_call x1, Pallas kernels, exchange_call(): pl.pallas_call(functools.partial(exchange_kernel, nx, ny), out_shape=(jax...  39 us

profile of v3, /device:TPU:32, one launch (start us, length us, event | category | flops | bytes accessed | tf_op | source)
XLA Modules:
  0.0 130.5 jit_solution(16471849834048572522)
XLA Ops:
  0.0 0.0 copy-start.2
  0.0 0.0 copy-start.3
  0.0 0.0 copy-start.7
  0.0 1.1 copy_bitcast_fusion
  1.1 0.0 copy-start.6
  1.1 0.0 copy-start.8
  1.1 0.0 copy-done.2
  1.1 0.0 copy-done.3
  1.1 0.0 copy-done.7
  1.2 0.6 copy-done.6
  1.8 0.0 copy-done.8
  1.8 0.0 copy-start.5
  1.8 39.0 %shard_map.109 = (f32[192,8,128]{2,1,0:T(8,128)S(1)}, f32[8,8192]{1,0:T(8,128)S(1)}) custom-call(f32[3,8192]{1,0:T(4,128)S(1)} %get-tuple-element.10.off_ref, f32[3,8192]{1,0:T(4,128)S(1)} %get-tuple-element.9.line_ref, s32[1,8192]{1,0:T(1,128)S(1)} %bitcast.18, s32[1,8192]{1,0:T(1,128)S(1)} %bitcast.19, f32[6]{0:T(128)S(1)} %copy-done.8, ...), custom_call_target="tpu_custom_call" | custom-call | tf_op jit(solution)/shard_map/pallas_call | solution.py:695
  40.8 0.0 copy-done.5
  40.8 0.0 copy-start
  40.8 0.0 copy-start.1
  40.8 0.0 copy-start.4
  40.8 39.1 %shard_map.110.half_ref = f32[512,128]{1,0:T(8,128)S(1)} custom-call(s32[2,1024]{1,0:T(2,128)S(1)} %bitcast.21, f32[1536,128]{1,0:T(8,128)S(1)} %bitcast.14, f32[8,8192]{1,0:T(8,128)S(1)} %get-tuple-element.8.base_ref), custom_call_target="tpu_custom_call" | custom-call | tf_op jit(solution)/shard_map/pallas_call | solution.py:270
  80.0 0.0 copy-done
  80.0 0.0 copy-done.1
  80.0 0.0 copy-done.4
  80.0 49.7 %shard_map.111 = f32[3,8192]{1,0:T(4,128)S(1)} custom-call(f32[512,128]{1,0:T(8,128)S(1)} %shard_map.110.half_ref, s32[2,8192]{1,0:T(2,128)S(1)} %bitcast.16, s32[2,8192]{1,0:T(2,128)S(1)} %bitcast.17, f32[1,8192]{1,0:T(1,128)S(1)} %bitcast.20), custom_call_target="tpu_custom_call" | custom-call | tf_op jit(solution)/shard_map/pallas_call | solution.py:868
  129.7 0.7 copy.12
Async XLA Ops:
  0.0 1.1 copy-start.2
  0.0 1.1 copy-start.3
  0.0 1.1 copy-start.7
  1.1 0.7 copy-start.6
  1.1 0.7 copy-start.8
  1.8 39.0 %copy-start.5 = (s32[1,1,2,1024]{3,2,1,0:T(2,128)S(1)}, s32[1,1,2,1024]{3,2,1,0:T(2,128)}, u32[]{:S(2)}) copy-start(s32[1,1,2,1024]{3,2,1,0:T(2,128)} %param.19) | copy-start | bytes 24580
  40.8 39.2 %copy-start = (s32[1,1,2,8192]{3,2,1,0:T(2,128)S(1)}, s32[1,1,2,8192]{3,2,1,0:T(2,128)}, u32[]{:S(2)}) copy-start(s32[1,1,2,8192]{3,2,1,0:T(2,128)} %param.15) | copy-start | bytes 196612
  40.8 39.2 %copy-start.1 = (s32[1,1,2,8192]{3,2,1,0:T(2,128)S(1)}, s32[1,1,2,8192]{3,2,1,0:T(2,128)}, u32[]{:S(2)}) copy-start(s32[1,1,2,8192]{3,2,1,0:T(2,128)} %param.16) | copy-start | bytes 196612
  40.8 39.2 %copy-start.4 = (f32[1,1,8192]{2,1,0:T(1,128)S(1)}, f32[1,1,8192]{2,1,0:T(1,128)}, u32[]{:S(2)}) copy-start(f32[1,1,8192]{2,1,0:T(1,128)} %param.17) | copy-start | bytes 98308

commit v4 on v3

--- a/solution.py
+++ b/solution.py
@@ -33,7 +33,7 @@
     ((1.0, 0, (0, 1, 2)), (1.0, 1, (1, 1, 2)), (-1.0, 2, (0, 0, 1)), (-1.0, 2, (1, 1, 1))),
 )
 CENTER = (CCX / 2.0, CCY / 2.0, NCZ / 2.0)
-UNROLL = 32
+UNROLL = 64
 PAIR_STEP = 256
 TRANSPOSED = (((1,), (1,)), ((), ()))
 f32 = jnp.float32
@@ -351,7 +351,7 @@
     all_send,
     all_recv,
 ):
-    segs = off_ref.shape[1]
+    segs = cell_ref.shape[1]
     blocks = segs // SEG
     packet = listx_ref.shape[1]
     cells = hot.shape[0]
@@ -396,11 +396,14 @@
         lanes = pl.ds(pl.multiple_of(block * SEG, SEG), SEG)
         cell = cell_ref[:, lanes]
         kind = kind_ref[:, lanes]
-        dline = line_ref[:, lanes]
-        shift = off_ref[:, lanes]
+        spots = [
+            pl.ds(pl.multiple_of(axis * segs + block * SEG, SEG), SEG) for axis in range(3)
+        ]
+        dline = jnp.concatenate([line_ref[:, where] for where in spots], axis=0)
         corner = (cell // (CCY * NCZ), cell // NCZ % CCY, cell % NCZ)
         place = [
-            (corner[axis].astype(f32) + origin[axis]) + shift[axis : axis + 1] for axis in range(3)
+            (corner[axis].astype(f32) + origin[axis]) + off_ref[:, spots[axis]]
+            for axis in range(3)
         ]
         code = kind.astype(f32)
         gh_ref[block] = jnp.concatenate(
@@ -445,9 +448,6 @@
                 device_id_type=mesh_ids,
             )
         )
-    for copy in copies_x:
-        copy.start()
-
     def row_copy(step):
         return pltpu.make_async_remote_copy(
             src_ref=mine,
@@ -467,41 +467,10 @@
         return carry
 
     lax.fori_loop(1, depth_count, row_start, 0)
+    for copy in copies_x:
+        copy.start()
 
     row_iota = lax.broadcasted_iota(jnp.int32, (8, SEG), 0)
-    for copy in copies_x:
-        copy.wait()
-    for slot in range(2):
-        moved = jnp.where(row_iota == 0, -float(CCX) if slot == 0 else float(CCX), 0.0)
-
-        def take_x(item, carry, slot=slot, moved=moved):
-            gh_ref[blocks + slot * packet + item] = land_x[slot, item] + moved
-            return carry
-
-        lax.fori_loop(0, packet, take_x, 0, unroll=8)
-
-    def pick_y(item, carry):
-        for side in range(2):
-            source = listy_ref[side, item]
-            pack_y[side, item] = gh_ref[source]
-        return carry
-
-    lax.fori_loop(0, packet, pick_y, 0, unroll=8)
-    copies_y = []
-    for side in range(2):
-        target = lax.rem(me_y + (ny - 1 if side == 0 else 1), ny)
-        copies_y.append(
-            pltpu.make_async_remote_copy(
-                src_ref=pack_y.at[side],
-                dst_ref=land_y.at[1 - side],
-                send_sem=sem_y.at[side],
-                recv_sem=sem_y.at[2 + side],
-                device_id=(me_x, target),
-                device_id_type=mesh_ids,
-            )
-        )
-    for copy in copies_y:
-        copy.start()
 
     lax.fori_loop(1, depth_count, row_wait, 0)
     lane_iota = lax.broadcasted_iota(jnp.int32, (16, SEG), 1)
@@ -539,17 +508,6 @@
 
     lax.fori_loop(1, half_x // 2, all_start, 0)
     all_copy(half_x // 2).start()
-
-    for copy in copies_y:
-        copy.wait()
-    for slot in range(2):
-        moved = jnp.where(row_iota == 1, -float(CCY) if slot == 0 else float(CCY), 0.0)
-
-        def take_y(item, carry, slot=slot, moved=moved):
-            gh_ref[blocks + (2 + slot) * packet + item] = land_y[slot, item] + moved
-            return carry
-
-        lax.fori_loop(0, packet, take_y, 0, unroll=8)
 
     far_acc[...] = jnp.zeros_like(far_acc)
 
@@ -652,6 +610,42 @@
         return carry
 
     lax.fori_loop(0, 8, far_own, 0)
+
+    for copy in copies_x:
+        copy.wait()
+    for slot in range(2):
+        moved = jnp.where(row_iota == 0, -float(CCX) if slot == 0 else float(CCX), 0.0)
+
+        def take_x(item, carry, slot=slot, moved=moved):
+            gh_ref[blocks + slot * packet + item] = land_x[slot, item] + moved
+            return carry
+
+        lax.fori_loop(0, packet, take_x, 0, unroll=8)
+
+    def pick_y(item, carry):
+        for side in range(2):
+            source = listy_ref[side, item]
+            pack_y[side, item] = gh_ref[source]
+        return carry
+
+    lax.fori_loop(0, packet, pick_y, 0, unroll=8)
+    copies_y = []
+    for side in range(2):
+        target = lax.rem(me_y + (ny - 1 if side == 0 else 1), ny)
+        copies_y.append(
+            pltpu.make_async_remote_copy(
+                src_ref=pack_y.at[side],
+                dst_ref=land_y.at[1 - side],
+                send_sem=sem_y.at[side],
+                recv_sem=sem_y.at[2 + side],
+                device_id=(me_x, target),
+                device_id_type=mesh_ids,
+            )
+        )
+    for copy in copies_y:
+        copy.start()
+
+
     lax.fori_loop(1, half_x // 2, far_columns, 0)
     all_copy(half_x // 2).wait_recv()
     lax.fori_loop(0, 4, far_last, 0)
@@ -683,9 +677,20 @@
 
     lax.fori_loop(0, segs // width, base_step, 0)
 
+    for copy in copies_y:
+        copy.wait()
+    for slot in range(2):
+        moved = jnp.where(row_iota == 1, -float(CCY) if slot == 0 else float(CCY), 0.0)
+
+        def take_y(item, carry, slot=slot, moved=moved):
+            gh_ref[blocks + (2 + slot) * packet + item] = land_y[slot, item] + moved
+            return carry
+
+        lax.fori_loop(0, packet, take_y, 0, unroll=8)
+
 
 def exchange_call(nx, ny, offsets, dline, kind, cell, applied, list_x, list_y):
-    segs = offsets.shape[1]
+    segs = cell.shape[1]
     blocks = segs // SEG
     packet = list_x.shape[1]
     number = blocks + 4 * packet
@@ -855,10 +860,10 @@
     )
     scale = 1.0 / (drag * (sums[3] + CORE_LENGTH))
     speed = [sums[item] * scale for item in range(3)]
-    for row in range(rows):
-        out_ref[:, row * NODE_COLS : (row + 1) * NODE_COLS] = jnp.concatenate(
-            [piece[row : row + 1] for piece in speed], axis=0
-        )
+    for item in range(3):
+        for row in range(rows):
+            first = (item * rows + row) * NODE_COLS
+            out_ref[:, first : first + NODE_COLS] = speed[item][row : row + 1]
 
 
 def nodal_call(nx, ny, half, node, owner, drag):
@@ -867,7 +872,7 @@
     vmem = pl.BlockSpec(memory_space=pltpu.VMEM)
     return pl.pallas_call(
         functools.partial(nodal_kernel, nx, ny),
-        out_shape=jax.ShapeDtypeStruct((3, drag.shape[1]), f32),
+        out_shape=jax.ShapeDtypeStruct((1, 3 * drag.shape[1]), f32),
         in_specs=[vmem] * 4,
         out_specs=vmem,
         scratch_shapes=[
@@ -904,8 +909,8 @@
     ghosts, base = exchange_call(
         nx,
         ny,
-        offsets[0, 0],
-        line[0, 0],
+        offsets.reshape(1, -1),
+        line.reshape(1, -1),
         burgers_kind[0],
         seg_cell[0],
         applied,
@@ -914,7 +919,7 @@
     )
     half = near_call(pairs, ghosts.reshape(-1, SEG), base)
     velocity = nodal_call(nx, ny, half, end_node[0, 0], end_owner[0, 0], drag[0])
-    return velocity[None, None]
+    return velocity.reshape(1, 1, 3, -1)
 
 
 def solution(mesh):

time: 131 us -> 127 us (0.969)
  the two profiles are of different devices: /device:TPU:32 before, /device:TPU:65 now
where the time goes in v4:
time: 127 us
  Pallas kernels  122 us (96%)
  local copies, waits for them, and re-layouts  4.66 us (4%)
    pallas_call x1, Pallas kernels, nodal_call(): pl.pallas_call(functools.partial(nodal_kernel, nx, ny), out_shape=jax.Sha...  47.4 us
    pallas_call x1, Pallas kernels, near_call(): pl.pallas_call(functools.partial(near_kernel, blocks, number), out_shape=...  38 us
    pallas_call x1, Pallas kernels, exchange_call(): pl.pallas_call(functools.partial(exchange_kernel, nx, ny), out_shape=(jax...  36.7 us
    unnamed x23, local copies, waits for them, and re-layouts  4.66 us

profile of v4, /device:TPU:65, one launch (start us, length us, event | category | flops | bytes accessed | tf_op | source)
XLA Modules:
  0.0 126.8 jit_solution(17589962480824027877)
XLA Ops:
  0.0 0.0 copy-start.9
  0.0 0.0 copy-start.8
  0.0 0.0 copy-start.10
  0.0 0.7 copy-done.9
  0.7 0.0 copy-done.8
  0.7 0.0 copy-done.10
  0.7 0.0 copy-start
  0.7 0.9 copy-done
  1.6 0.0 copy-start.1
  1.6 0.9 copy-done.1
  2.5 0.0 copy-start.5
  2.5 0.8 copy-done.5
  3.2 0.0 copy-start.6
  3.2 0.8 copy-done.6
  4.0 0.0 copy-start.7
  4.0 36.7 %shard_map.109 = (f32[192,8,128]{2,1,0:T(8,128)S(1)}, f32[8,8192]{1,0:T(8,128)S(1)}) custom-call(f32[1,24576]{1,0:T(1,128)S(1)} %bitcast.14, f32[1,24576]{1,0:T(1,128)S(1)} %bitcast.15, s32[1,8192]{1,0:T(1,128)S(1)} %bitcast.19, s32[1,8192]{1,0:T(1,128)S(1)} %bitcast.20, f32[6]{0:T(128)S(1)} %copy-done.10, s32[2,32]{1,0:T(2,128)S(1)} %bitcast.22, ...), custom_call_target="tpu_custom_call" | custom-call | tf_op jit(solution)/shard_map/pallas_call | solution.py:700
  40.7 0.0 copy-done.7
  40.7 0.0 copy-start.2
  40.7 0.0 copy-start.3
  40.7 0.0 copy-start.4
  40.8 38.0 %shard_map.110.half_ref = f32[512,128]{1,0:T(8,128)S(1)} custom-call(s32[2,1024]{1,0:T(2,128)S(1)} %bitcast.21, f32[1536,128]{1,0:T(8,128)S(1)} %bitcast.12, f32[8,8192]{1,0:T(8,128)S(1)} %get-tuple-element.8.base_ref), custom_call_target="tpu_custom_call" | custom-call | tf_op jit(solution)/shard_map/pallas_call | solution.py:270
  78.7 0.0 copy-done.2
  78.7 0.0 copy-done.3
  78.8 0.0 copy-done.4
  78.8 47.4 %shard_map.111 = f32[1,24576]{1,0:T(1,128)S(1)} custom-call(f32[512,128]{1,0:T(8,128)S(1)} %shard_map.110.half_ref, s32[2,8192]{1,0:T(2,128)S(1)} %bitcast.16, s32[2,8192]{1,0:T(2,128)S(1)} %bitcast.17, f32[1,8192]{1,0:T(1,128)S(1)} %bitcast.18), custom_call_target="tpu_custom_call" | custom-call | tf_op jit(solution)/shard_map/pallas_call | solution.py:873
  126.1 0.6 copy.15
Async XLA Ops:
  0.0 0.7 copy-start.9
  0.0 0.7 copy-start.8
  0.0 0.7 copy-start.10
  0.7 0.9 copy-start
  1.6 0.9 copy-start.1
  2.5 0.8 copy-start.5
  3.2 0.8 copy-start.6
  4.0 36.7 %copy-start.7 = (s32[1,1,2,1024]{3,2,1,0:T(2,128)S(1)}, s32[1,1,2,1024]{3,2,1,0:T(2,128)}, u32[]{:S(2)}) copy-start(s32[1,1,2,1024]{3,2,1,0:T(2,128)} %param.19) | copy-start | bytes 24580
  40.7 38.0 %copy-start.2 = (s32[1,1,2,8192]{3,2,1,0:T(2,128)S(1)}, s32[1,1,2,8192]{3,2,1,0:T(2,128)}, u32[]{:S(2)}) copy-start(s32[1,1,2,8192]{3,2,1,0:T(2,128)} %param.15) | copy-start | bytes 196612
  40.7 38.0 %copy-start.3 = (s32[1,1,2,8192]{3,2,1,0:T(2,128)S(1)}, s32[1,1,2,8192]{3,2,1,0:T(2,128)}, u32[]{:S(2)}) copy-start(s32[1,1,2,8192]{3,2,1,0:T(2,128)} %param.16) | copy-start | bytes 196612
  40.7 38.0 %copy-start.4 = (f32[1,1,8192]{2,1,0:T(1,128)S(1)}, f32[1,1,8192]{2,1,0:T(1,128)}, u32[]{:S(2)}) copy-start(f32[1,1,8192]{2,1,0:T(1,128)} %param.17) | copy-start | bytes 98308

commit v5 on v4

--- a/solution.py
+++ b/solution.py
@@ -154,11 +154,20 @@
                 ).astype(bf16)
         return carry
 
+    row = lax.broadcasted_iota(jnp.int32, (16, 3 * SEG), 0)
+    lane = lax.broadcasted_iota(jnp.int32, (16, 3 * SEG), 1)
+    choose = jnp.where((row < 9) & (row % 3 == lane // SEG), 1.0, 0.0).astype(bf16)
+
     def target_step(block):
         tile = gh_ref[pl.ds(pl.multiple_of(block * 8, 8), 8), :]
-        columns = jnp.transpose(tile)
+        parts = jnp.concatenate(
+            [piece[0:3] for piece in parts_of(tile)] + [jnp.zeros((7, SEG), f32)], axis=0
+        ).astype(bf16)
+        spread = lax.dot_general(
+            parts, choose, (((0,), (0,)), ((), ())), preferred_element_type=f32
+        )
         for axis in range(3):
-            xb[3 * block + axis] = jnp.broadcast_to(columns[:, axis : axis + 1], (SEG, SEG))
+            xb[3 * block + axis] = spread[:, axis * SEG : (axis + 1) * SEG]
         acc[block] = zero
 
     def both_step(group, carry):
@@ -318,6 +327,9 @@
         "bz": BULK_TERM * curl_both[2],
         "sx": BULK_TERM * step * step * curl_both[0],
     }
+    curls["ox2"] = 2.0 * curls["ox"]
+    curls["by2"] = 2.0 * curls["by"]
+    curls["bz2"] = 2.0 * curls["bz"]
     return turned, curls
 
 
@@ -396,14 +408,11 @@
         lanes = pl.ds(pl.multiple_of(block * SEG, SEG), SEG)
         cell = cell_ref[:, lanes]
         kind = kind_ref[:, lanes]
-        spots = [
-            pl.ds(pl.multiple_of(axis * segs + block * SEG, SEG), SEG) for axis in range(3)
-        ]
-        dline = jnp.concatenate([line_ref[:, where] for where in spots], axis=0)
+        dline = line_ref[:, lanes]
+        shift = off_ref[:, lanes]
         corner = (cell // (CCY * NCZ), cell // NCZ % CCY, cell % NCZ)
         place = [
-            (corner[axis].astype(f32) + origin[axis]) + off_ref[:, spots[axis]]
-            for axis in range(3)
+            (corner[axis].astype(f32) + origin[axis]) + shift[axis : axis + 1] for axis in range(3)
         ]
         code = kind.astype(f32)
         gh_ref[block] = jnp.concatenate(
@@ -555,18 +564,20 @@
                 inv_two = inv_one * inv_one
                 inv_three = jnp.where(keep, 0.0, inv_two * inv_one)
                 inv_five = inv_three * inv_two
-                gain = 2.0 * inv_three + (3.0 * CORE_SQUARE) * inv_five
+                fifth = (3.0 * CORE_SQUARE) * inv_five
+                middle_gain = inv_three + fifth
+                gain = inv_three + middle_gain
                 dot_both = curls["ox"] + ry * curls["by"] + rz * curls["bz"]
                 dot_odd = curls["sx"] + ry * curls["oy"] + rz * curls["oz"]
-                trace = (inv_three + (3.0 * CORE_SQUARE) * inv_five) * dot_both
+                trace = middle_gain * dot_both
                 thrice = 3.0 * inv_five
                 wave = thrice * dot_both
                 wave_odd = thrice * dot_odd
                 wave_y = wave * ry
                 bends = (
-                    2.0 * curls["ox"],
-                    2.0 * (ry * curls["by"]),
-                    2.0 * (rz * curls["bz"]),
+                    curls["ox2"],
+                    ry * curls["by2"],
+                    rz * curls["bz2"],
                     ry * curls["bx"] + curls["oy"],
                     rz * curls["bx"] + curls["oz"],
                     rz * curls["by"] + ry * curls["bz"],
@@ -909,8 +920,8 @@
     ghosts, base = exchange_call(
         nx,
         ny,
-        offsets.reshape(1, -1),
-        line.reshape(1, -1),
+        offsets[0, 0],
+        line[0, 0],
         burgers_kind[0],
         seg_cell[0],
         applied,

time: 127 us -> 122 us (0.961)
  the two profiles are of different devices: /device:TPU:65 before, /device:TPU:96 now
where the time goes in v5:
time: 122 us
  Pallas kernels  119 us (98%)
  local copies, waits for them, and re-layouts  2.41 us (2%)
    pallas_call x1, Pallas kernels, near_call(): pl.pallas_call(functools.partial(near_kernel, blocks, number), out_shape=...  48.6 us
    pallas_call x1, Pallas kernels, nodal_call(): pl.pallas_call(functools.partial(nodal_kernel, nx, ny), out_shape=jax.Sha...  37.3 us
    pallas_call x1, Pallas kernels, exchange_call(): pl.pallas_call(functools.partial(exchange_kernel, nx, ny), out_shape=(jax...  33.3 us

profile of v5, /device:TPU:96, one launch (start us, length us, event | category | flops | bytes accessed | tf_op | source)
XLA Modules:
  0.0 121.6 jit_solution(16137989770585111489)
XLA Ops:
  0.0 0.0 copy-start.2
  0.0 0.0 copy-start.3
  0.0 0.0 copy-start.7
  0.0 1.1 copy_bitcast_fusion
  1.1 0.0 copy-start.6
  1.1 0.0 copy-start.8
  1.1 0.0 copy-done.2
  1.1 0.0 copy-done.3
  1.1 0.0 copy-done.7
  1.2 0.6 copy-done.6
  1.8 0.0 copy-done.8
  1.8 0.0 copy-start.5
  1.8 33.3 %shard_map.109 = (f32[192,8,128]{2,1,0:T(8,128)S(1)}, f32[8,8192]{1,0:T(8,128)S(1)}) custom-call(f32[3,8192]{1,0:T(4,128)S(1)} %get-tuple-element.10.off_ref, f32[3,8192]{1,0:T(4,128)S(1)} %get-tuple-element.9.line_ref, s32[1,8192]{1,0:T(1,128)S(1)} %bitcast.18, s32[1,8192]{1,0:T(1,128)S(1)} %bitcast.19, f32[6]{0:T(128)S(1)} %copy-done.8, ...), custom_call_target="tpu_custom_call" | custom-call | tf_op jit(solution)/shard_map/pallas_call | solution.py:711
  35.1 0.0 copy-done.5
  35.1 0.0 copy-start
  35.1 0.0 copy-start.1
  35.1 0.0 copy-start.4
  35.1 48.6 %shard_map.110.half_ref = f32[512,128]{1,0:T(8,128)S(1)} custom-call(s32[2,1024]{1,0:T(2,128)S(1)} %bitcast.21, f32[1536,128]{1,0:T(8,128)S(1)} %bitcast.14, f32[8,8192]{1,0:T(8,128)S(1)} %get-tuple-element.8.base_ref), custom_call_target="tpu_custom_call" | custom-call | tf_op jit(solution)/shard_map/pallas_call | solution.py:279
  83.7 0.0 copy-done
  83.7 0.0 copy-done.1
  83.7 0.0 copy-done.4
  83.7 37.3 %shard_map.111 = f32[1,24576]{1,0:T(1,128)S(1)} custom-call(f32[512,128]{1,0:T(8,128)S(1)} %shard_map.110.half_ref, s32[2,8192]{1,0:T(2,128)S(1)} %bitcast.16, s32[2,8192]{1,0:T(2,128)S(1)} %bitcast.17, f32[1,8192]{1,0:T(1,128)S(1)} %bitcast.20), custom_call_target="tpu_custom_call" | custom-call | tf_op jit(solution)/shard_map/pallas_call | solution.py:884
  121.0 0.6 copy.19
Async XLA Ops:
  0.0 1.1 copy-start.2
  0.0 1.1 copy-start.3
  0.0 1.1 copy-start.7
  1.1 0.7 copy-start.6
  1.1 0.7 copy-start.8
  1.8 33.3 %copy-start.5 = (s32[1,1,2,1024]{3,2,1,0:T(2,128)S(1)}, s32[1,1,2,1024]{3,2,1,0:T(2,128)}, u32[]{:S(2)}) copy-start(s32[1,1,2,1024]{3,2,1,0:T(2,128)} %param.19) | copy-start | bytes 24580
  35.1 48.6 %copy-start = (s32[1,1,2,8192]{3,2,1,0:T(2,128)S(1)}, s32[1,1,2,8192]{3,2,1,0:T(2,128)}, u32[]{:S(2)}) copy-start(s32[1,1,2,8192]{3,2,1,0:T(2,128)} %param.15) | copy-start | bytes 196612
  35.1 48.6 %copy-start.1 = (s32[1,1,2,8192]{3,2,1,0:T(2,128)S(1)}, s32[1,1,2,8192]{3,2,1,0:T(2,128)}, u32[]{:S(2)}) copy-start(s32[1,1,2,8192]{3,2,1,0:T(2,128)} %param.16) | copy-start | bytes 196612
  35.1 48.6 %copy-start.4 = (f32[1,1,8192]{2,1,0:T(1,128)S(1)}, f32[1,1,8192]{2,1,0:T(1,128)}, u32[]{:S(2)}) copy-start(f32[1,1,8192]{2,1,0:T(1,128)} %param.17) | copy-start | bytes 98308

commit v6 on v5

--- a/solution.py
+++ b/solution.py
@@ -33,7 +33,7 @@
     ((1.0, 0, (0, 1, 2)), (1.0, 1, (1, 1, 2)), (-1.0, 2, (0, 0, 1)), (-1.0, 2, (1, 1, 1))),
 )
 CENTER = (CCX / 2.0, CCY / 2.0, NCZ / 2.0)
-UNROLL = 64
+UNROLL = 128
 PAIR_STEP = 256
 TRANSPOSED = (((1,), (1,)), ((), ()))
 f32 = jnp.float32
@@ -786,7 +786,7 @@
             column_hot[:, where] = (column_iota == column).astype(f32).astype(bf16)
         return carry
 
-    lax.fori_loop(0, segs // SEG, column_step, 0, unroll=2)
+    lax.fori_loop(0, segs // SEG, column_step, 0, unroll=4)
 
     tiles = CHUNK // SEG
     chunks = 2 * segs // CHUNK

time: 122 us -> 119 us (0.975)
  the two profiles are of different devices: /device:TPU:96 before, /device:TPU:94 now
where the time goes in v6:
time: 119 us; the launch traced here: 118 us
  Pallas kernels  115 us (97%)
  local copies, waits for them, and re-layouts  2.41 us (2%)
    pallas_call x1, Pallas kernels, nodal_call(): pl.pallas_call(functools.partial(nodal_kernel, nx, ny), out_shape=jax.Sha...  45.1 us
    pallas_call x1, Pallas kernels, near_call(): pl.pallas_call(functools.partial(near_kernel, blocks, number), out_shape=...  35.7 us
    pallas_call x1, Pallas kernels, exchange_call(): pl.pallas_call(functools.partial(exchange_kernel, nx, ny), out_shape=(jax...  34.5 us
    unnamed x20, local copies, waits for them, and re-layouts  2.41 us

profile of v6, /device:TPU:94, one launch (start us, length us, event | category | flops | bytes accessed | tf_op | source)
XLA Modules:
  0.0 117.9 jit_solution(18391051081806522123)
XLA Ops:
  0.0 0.0 copy-start.2
  0.0 0.0 copy-start.3
  0.0 0.0 copy-start.7
  0.0 1.1 copy_bitcast_fusion
  1.1 0.0 copy-start.6
  1.1 0.0 copy-start.8
  1.1 0.0 copy-done.2
  1.1 0.0 copy-done.3
  1.1 0.0 copy-done.7
  1.2 0.6 copy-done.6
  1.8 0.0 copy-done.8
  1.8 0.0 copy-start.5
  1.8 34.5 %shard_map.109 = (f32[192,8,128]{2,1,0:T(8,128)S(1)}, f32[8,8192]{1,0:T(8,128)S(1)}) custom-call(f32[3,8192]{1,0:T(4,128)S(1)} %get-tuple-element.10.off_ref, f32[3,8192]{1,0:T(4,128)S(1)} %get-tuple-element.9.line_ref, s32[1,8192]{1,0:T(1,128)S(1)} %bitcast.18, s32[1,8192]{1,0:T(1,128)S(1)} %bitcast.19, f32[6]{0:T(128)S(1)} %copy-done.8, ...), custom_call_target="tpu_custom_call" | custom-call | tf_op jit(solution)/shard_map/pallas_call | solution.py:711
  36.3 0.0 copy-done.5
  36.3 0.0 copy-start
  36.3 0.0 copy-start.1
  36.3 0.0 copy-start.4
  36.4 35.7 %shard_map.110.half_ref = f32[512,128]{1,0:T(8,128)S(1)} custom-call(s32[2,1024]{1,0:T(2,128)S(1)} %bitcast.21, f32[1536,128]{1,0:T(8,128)S(1)} %bitcast.14, f32[8,8192]{1,0:T(8,128)S(1)} %get-tuple-element.8.base_ref), custom_call_target="tpu_custom_call" | custom-call | tf_op jit(solution)/shard_map/pallas_call | solution.py:279
  72.1 0.0 copy-done
  72.1 0.0 copy-done.1
  72.1 0.0 copy-done.4
  72.1 45.1 %shard_map.111 = f32[1,24576]{1,0:T(1,128)S(1)} custom-call(f32[512,128]{1,0:T(8,128)S(1)} %shard_map.110.half_ref, s32[2,8192]{1,0:T(2,128)S(1)} %bitcast.16, s32[2,8192]{1,0:T(2,128)S(1)} %bitcast.17, f32[1,8192]{1,0:T(1,128)S(1)} %bitcast.20), custom_call_target="tpu_custom_call" | custom-call | tf_op jit(solution)/shard_map/pallas_call | solution.py:884
  117.3 0.6 copy.19
Async XLA Ops:
  0.0 1.1 copy-start.2
  0.0 1.1 copy-start.3
  0.0 1.1 copy-start.7
  1.1 0.7 copy-start.6
  1.1 0.7 copy-start.8
  1.8 34.5 %copy-start.5 = (s32[1,1,2,1024]{3,2,1,0:T(2,128)S(1)}, s32[1,1,2,1024]{3,2,1,0:T(2,128)}, u32[]{:S(2)}) copy-start(s32[1,1,2,1024]{3,2,1,0:T(2,128)} %param.19) | copy-start | bytes 24580
  36.3 35.8 %copy-start = (s32[1,1,2,8192]{3,2,1,0:T(2,128)S(1)}, s32[1,1,2,8192]{3,2,1,0:T(2,128)}, u32[]{:S(2)}) copy-start(s32[1,1,2,8192]{3,2,1,0:T(2,128)} %param.15) | copy-start | bytes 196612
  36.3 35.8 %copy-start.1 = (s32[1,1,2,8192]{3,2,1,0:T(2,128)S(1)}, s32[1,1,2,8192]{3,2,1,0:T(2,128)}, u32[]{:S(2)}) copy-start(s32[1,1,2,8192]{3,2,1,0:T(2,128)} %param.16) | copy-start | bytes 196612
  36.3 35.8 %copy-start.4 = (f32[1,1,8192]{2,1,0:T(1,128)S(1)}, f32[1,1,8192]{2,1,0:T(1,128)}, u32[]{:S(2)}) copy-start(f32[1,1,8192]{2,1,0:T(1,128)} %param.17) | copy-start | bytes 98308
